TPU v7x, 32 devices: a whole 2x2x4 slice. The times are simulated.
32 devices in a mesh: trench: 8 (over y, x, core), tblock: 4 (over z).
Axes of the slice: x: 2, y: 2, z: 4, core: 2. Of those that a mesh axis runs over, the one named last changes fastest.
Arguments:
- adjoint_eta: float32 [4, 30, 128, 512], P('tblock', None, 'trench'), may hold values from -6 to 6
- adjoint_flow: float32 [4, 30, 128, 512], P('tblock', None, 'trench'), may hold values from -6 to 6
- residual: float32 [4, 8, 8, 4, 32], P('tblock', 'trench'), may hold values from -6 to 6
- sensor_cell: int32 [8, 8, 32], replicated, may hold values from 0 to 8191
- sensor_count: int32 [8, 8], replicated, may hold values from 0 to 32, as said below
- depth_class: int32 [128, 512], P('trench'), may hold values from 0 to 7
- speed_table: float32 [8], replicated, may hold values from 0.1 to 0.3
- damping: float32 [30], replicated, may hold values from 0.6 to 1
- profile: float32 [30], replicated, may hold values from 0.3 to 1
- band_weight: float32 [8], replicated, may hold values from 0.3 to 1
Outputs:
- uplift_grad: float32 [16, 128, 512], P(None, ('trench', 'tblock'))
Inputs may be any that keep to these rules, and one draw needn't show every extreme that they name: `sensor_cell`: column index inside the owning tile, row times 512 plus column. `sensor_count`: in every draw some owning tile receives 32 live slots from every source tile.
All inputs are finite; a program needn't handle non-finite values.
Results may differ from a plain program's by a relative error of at most 0.0001.
Values sent between devices are 32-bit elements; how exact they have to be, the bound alone decides.
No kernel may reach another device: no remote copies, remote signals or barrier semaphores. Data moves between devices by JAX's collectives and lax.ppermute only.
A program may use at most 64 MiB of HBM per device.

v0:
```python
import functools
import math

import jax
import jax.numpy as jnp
from jax import lax
from jax.experimental import pallas as pl
from jax.experimental.pallas import tpu as pltpu
from jax.sharding import PartitionSpec as P

VERT = 0.2
STEPS = 4
PAD = 8
VMEM = pltpu.VMEM
SMEM = pltpu.SMEM
LIMIT = 32 * 1024 * 1024

SHIFT = 1.2

FIELDS = [(4, 4), (4, 3), (4, 2), (3, 2), (4, 1), (3, 1), (2, 1), (4, 0), (3, 0), (2, 0), (1, 0)]
HALO = [4, 3, 2, 2, 1, 1, 1]
HALO_AT = [0, 4, 7, 9, 11, 12, 13]
CEL_AT = 14
CEL_HALO = 3
ROWS = 17


def split(x):
    hi = x.astype(jnp.bfloat16)
    return hi, (x - hi.astype(jnp.float32)).astype(jnp.bfloat16)


def dot(a, b, dims=((1,), (0,))):
    return lax.dot_general(a, b, (dims, ((), ())), preferred_element_type=jnp.float32)


def prepare_kernel(
    depth, table, damping, profile, band, residual, eta, flow,
    w_eta, w_flow, cel, coef, factor, own, eta_v, flow_v,
    depth_v, table_s, damping_v, profile_v, band_v, sems,
):
    rows, across = cel.shape
    levels = damping.shape[1]
    copies = [
        pltpu.make_async_copy(src, dst, sems.at[i])
        for i, (src, dst) in enumerate((
            (damping, damping_v), (profile, profile_v), (table, table_s), (depth, depth_v),
            (band, band_v), (residual, own), (eta, eta_v), (flow, flow_v),
        ))
    ]
    for copy in copies:
        copy.start()
    for copy in copies[:-2]:
        copy.wait()

    classes = depth_v[...]
    speed = jnp.zeros(classes.shape, jnp.float32)
    for c in range(table_s.shape[0]):
        speed = jnp.where(classes == c, table_s[c], speed)
    cel[...] = speed
    for j in range(factor.shape[0]):
        factor[j : j + 1, :] = jnp.broadcast_to(band_v[:, j : j + 1], (1, across))

    lane = lax.broadcasted_iota(jnp.int32, (8, 128), 1)
    sub = lax.broadcasted_iota(jnp.int32, (8, 128), 0)
    inside = lane < levels
    fill = jnp.zeros((1, 128 - levels), jnp.float32)
    keep = jnp.broadcast_to(jnp.concatenate([damping_v[...], fill], axis=1), (8, 128))
    weight = jnp.broadcast_to(jnp.concatenate([profile_v[...], fill], axis=1), (8, 128))
    u = jnp.zeros((8, 128), jnp.float32)
    v = jnp.where(sub == 0, weight * (1.0 / math.sqrt(levels)), 0.0)
    us, vs = [u], [v]
    for r in range(STEPS):
        s = u + v
        bottom = jnp.sum(jnp.where(lane == levels - 1, s, 0.0), axis=1, keepdims=True)
        coef[8 * r : 8 * r + 8, :] = jnp.broadcast_to(bottom, (8, coef.shape[1]))
        vertical = pltpu.roll(s, 1, 1) + pltpu.roll(s, 127, 1) - 2.0 * s
        u = jnp.where(inside, u + VERT * vertical - SHIFT * s + pltpu.roll(s, 1, 0), 0.0)
        v = s * keep
        us.append(u)
        vs.append(v)

    wide = w_eta.shape[1]
    spread = (
        lax.broadcasted_iota(jnp.int32, (128, wide), 1) // 8
        == lax.broadcasted_iota(jnp.int32, (128, wide), 0)
    ).astype(jnp.bfloat16)
    count_f = len(FIELDS) + 1
    diagonal = (
        lax.broadcasted_iota(jnp.int32, (8 * count_f, wide), 1) % 8
        == lax.broadcasted_iota(jnp.int32, (8 * count_f, wide), 0) % 8
    )

    def matrix(vectors):
        blocks = [jnp.broadcast_to(vectors[n][k : k + 1, :], (8, 128)) for n, k in FIELDS]
        blocks.append(jnp.zeros((8, 128), jnp.float32))
        hi, lo = split(jnp.concatenate(blocks, axis=0))
        zero = jnp.zeros((8 * count_f, wide), jnp.float32)
        hi = jnp.where(diagonal, dot(hi, spread), zero).astype(jnp.bfloat16)
        lo = jnp.where(diagonal, dot(lo, spread), zero).astype(jnp.bfloat16)
        return jnp.concatenate([hi, lo], axis=0)

    w_eta[...] = matrix(us)
    w_flow[...] = matrix(vs)

    for copy in copies[-2:]:
        copy.wait()


def contract_kernel(eta, flow, w_eta, w_flow, cel, own, partner, fields, inner, outer, *relays):
    levels, rows, across = eta.shape[1:]
    wide = w_eta.shape[1]
    half = w_eta.shape[0] // 2
    for h in range(rows // 8):
        hi, lo = split(eta[0, :, 8 * h : 8 * h + 8, :].reshape(wide, across))
        total = dot(w_eta[...], hi)
        part = dot(w_eta[0:half, :], lo)
        hi, lo = split(flow[0, :, 8 * h : 8 * h + 8, :].reshape(wide, across))
        total += dot(w_flow[...], hi)
        part += dot(w_flow[0:half, :], lo)
        part = part + total[:half] + total[half:]
        for f in range(len(FIELDS)):
            fields[f, 8 * h : 8 * h + 8, :] = part[8 * f : 8 * f + 8]

    me = lax.axis_index("trench")
    tiles = own.shape[0]
    for d in range(1, len(relays) + 2):
        target = met(me, d, tiles)
        values = [both_rows(target, own, partner)]
        if d <= passed_on(tiles):
            values.append(both_rows(target ^ 1, own, partner))
        out = relays[d - 2] if d > 1 else outer
        out[0:STEPS, :] = widen(values, out.shape[1])

    def edge(out, at, last):
        for f, width in enumerate(HALO):
            start = rows - width if last else 0
            out[at + HALO_AT[f] : at + HALO_AT[f] + width, :] = fields[f, start : start + width, :]
        start = rows - CEL_HALO if last else 0
        out[at + CEL_AT : at + CEL_AT + CEL_HALO, :] = cel[start : start + CEL_HALO, :]

    @pl.when(me % 2 == 0)
    def _():
        edge(inner, 0, True)
        edge(outer, STEPS, False)

    @pl.when(me % 2 == 1)
    def _():
        edge(inner, 0, False)
        edge(outer, STEPS, True)


def met(me, d, tiles):
    odd = me % 2
    chip = (me // 2 + jnp.where(odd == 1, d, tiles // 2 - d)) % (tiles // 2)
    return jnp.where(d == 0, me, 2 * chip + 1 - odd)


def direct(tiles):
    return tiles // 4


def passed_on(tiles):
    return tiles // 2 - 1 - direct(tiles)


def sources(me, tiles):
    near = [met(me, d, tiles) ^ core for d in range(direct(tiles) + 1) for core in range(2)]
    far = [met(me ^ 1, d, tiles) ^ core for d in range(1, passed_on(tiles) + 1) for core in range(2)]
    return near, far


def packed(q):
    return STEPS * (q // 2), 256 * (q % 2)


def widen(values, lanes):
    fill = lanes - sum(value.shape[1] for value in values)
    if fill:
        values = values + [jnp.zeros((STEPS, fill), jnp.float32)]
    return jnp.concatenate(values, axis=1)


def residual_rows(owner, own):
    tiles = own.shape[0]
    return jnp.concatenate([own[jnp.clip(owner + d - 1, 0, tiles - 1)] for d in range(3)], axis=1)


def both_rows(owner, own, partner):
    return jnp.concatenate([residual_rows(owner, own), residual_rows(owner, partner)], axis=1)


def pass_kernel(slots, count, inner, after, *refs):
    gots, out = refs[:-1], refs[-1]
    per = 6 * slots
    top = out.shape[0] - ROWS
    out[0:top, :] = jnp.zeros((top, out.shape[1]), jnp.float32)
    for q in range(count):
        row, lane = packed(q)
        out[row : row + STEPS, lane : lane + 256] = widen([gots[q][0:STEPS, per : 2 * per]], 256)
    out[top:, :] = inner[...]


def sensors_kernel(rows, cells, count, hot_early, places_early, hot_late, places_late):
    me = lax.axis_index("trench")
    tiles, _, slots = cells.shape
    across = hot_early.shape[0]
    slot = lax.broadcasted_iota(jnp.int32, (1, slots), 1)
    bits = across.bit_length() - 1

    def list_slots(listed_sources, hot, places):
        listed = []
        for source in listed_sources:
            for d in range(3):
                owner = me + d - 1
                inside = (owner >= 0) & (owner < tiles)
                owner = jnp.clip(owner, 0, tiles - 1)
                live = jnp.where(inside, count[source, owner], 0)
                listed.append(jnp.where(slot < live, cells[source, pl.ds(owner, 1), :], -1))
        listed = jnp.concatenate(listed, axis=1)
        tile = (lax.broadcasted_iota(jnp.int32, listed.shape, 1) // slots) % 3
        at = jnp.where(listed < 0, -1, (listed >> bits) + (rows * (tile - 1) + PAD))
        places[...] = jnp.broadcast_to(at, places.shape)
        columns = listed & (across - 1)
        hot[...] = jnp.where(lax.broadcasted_iota(jnp.int32, hot.shape, 0) == columns, 1.0, 0.0).astype(jnp.bfloat16)

    early, late = sources(me, tiles)
    list_slots(early, hot_early, places_early)
    list_slots(late, hot_late, places_late)


def planes_of(values, hot, places, tall):
    here = lax.broadcasted_iota(jnp.int32, (tall, values.shape[1]), 0) == places[0:1, :]
    left = jnp.concatenate([jnp.where(here, values[t : t + 1, :], 0.0) for t in range(STEPS)], axis=0)
    both = dot(jnp.concatenate(split(left), axis=0), hot[...], ((1,), (1,)))
    return both[: STEPS * tall] + both[STEPS * tall :]


def inject_kernel(hot, places, own, partner, *refs):
    gots, planes = refs[:-1], refs[-1]
    per = 6 * own.shape[2]
    values = [both_rows(lax.axis_index("trench"), own, partner)] + [got[0:STEPS, 0:per] for got in gots]
    planes[...] = planes_of(jnp.concatenate(values, axis=1), hot, places, planes.shape[0] // STEPS)


def advance_kernel(tiles, fields, cel, coef, hot, places, facing_in, facing_out, planes, *refs):
    outs, (stage, ext, cel_ext) = refs[:-3], refs[-3:]
    blocks = len(outs)
    me = lax.axis_index("trench")
    rows, across = cel.shape
    tall = rows + 2 * PAD
    part = rows // blocks
    odd = me % 2 == 1
    facing = me // 2 + jnp.where(odd, 1, -1)
    top = facing_in.shape[0] - ROWS
    inner = facing_in[top:, :]
    outer = jnp.where((facing >= 0) & (facing < tiles // 2), facing_out[STEPS:, :], 0.0)
    before = jnp.where(odd, inner, outer)
    after = jnp.where(odd, outer, inner)

    count = passed_on(tiles)
    per = hot.shape[1] // count
    late = [facing_in[row : row + STEPS, at : at + per] for row, at in map(packed, range(count))]
    all_planes = planes[...] + planes_of(jnp.concatenate(late, axis=1), hot, places, tall)
    inject = [all_planes[tall * t : tall * t + tall] for t in range(STEPS)]

    def extend(store, own, at, width):
        store(0, PAD, jnp.zeros((PAD, across), jnp.float32))
        store(PAD + rows, tall, jnp.zeros((PAD, across), jnp.float32))
        store(PAD, PAD + rows, own)
        store(PAD - width, PAD, before[at : at + width])
        store(PAD + rows, PAD + rows + width, after[at : at + width])

    for f, width in enumerate(HALO):
        def store(a, b, value, f=f):
            ext[f, a:b, :] = value
        extend(store, fields[f], HALO_AT[f], width)

    def store_cel(a, b, value):
        cel_ext[a:b, :] = value
    extend(store_cel, cel[...], CEL_AT, CEL_HALO)

    lane = lax.broadcasted_iota(jnp.int32, (tall, across), 1)
    first = lane == 0
    last = lane == across - 1
    speed = cel_ext[...]

    def horizontal(z):
        around = pltpu.roll(z, 1, 0) + pltpu.roll(z, tall - 1, 0)
        around += jnp.where(first, 0.0, pltpu.roll(z, 1, 1))
        around += jnp.where(last, 0.0, pltpu.roll(z, across - 1, 1))
        return speed * (around - 4.0 * z) + SHIFT * z

    def injected(n, k, a, b):
        total = None
        for tau in range(1, n - k + 1):
            r = n - tau
            term = coef[8 * r + k : 8 * r + k + 1, :] * inject[STEPS - tau][a:b]
            total = term if total is None else total + term
        return total

    base = horizontal(ext[0])
    for n in range(1, STEPS + 1):
        z = base
        for k in range(n - 1, 0, -1):
            z = horizontal(z + ext[FIELDS.index((n, k))] + injected(n, k, 0, tall))
        own = z[PAD : PAD + rows] + fields[FIELDS.index((n, 0))] + injected(n, 0, PAD, PAD + rows)
        t = STEPS - n
        for b in range(blocks):
            stage[b, part * t : part * t + part, :] = own[part * b : part * b + part]
    block = lax.axis_index("tblock")
    for r, out in enumerate(outs):
        out[...] = stage[block ^ r]


def prior_kernel(*refs):
    gots, (weight, out, whole, done, sems) = refs[:-5], refs[-5:]
    block = lax.axis_index("tblock")
    for r, got in enumerate(reversed(gots)):
        whole[block ^ r] = got[...]
    part = out.shape[1]
    length = out.shape[0]
    width = weight.shape[0]
    factor = [weight[j : j + 1, :] for j in range(width)]
    copies = []

    def finish(p):
        if (p + 1) % (length // 4) == 0:
            cut = pl.ds(p + 1 - length // 4, length // 4)
            copies.append(pltpu.make_async_copy(done.at[cut], out.at[cut], sems.at[len(copies)]))
            copies[-1].start()

    if 2 * part != 8:
        series = [whole[i // STEPS, part * (i % STEPS) : part * (i % STEPS) + part, :] for i in range(length)]
        for k in range(length):
            done[k] = sum(factor[j] * series[k + j] for j in range(min(width, length - k)))
            finish(k)
        for copy in copies:
            copy.wait()
        return
    pairs = length // 2
    even = [whole[p // 2, 8 * (p % 2) : 8 * (p % 2) + 8, :] for p in range(pairs)]
    half = lax.broadcasted_iota(jnp.int32, even[0].shape, 0) < part
    turned = [pltpu.roll(x, part, 0) for x in even] + [jnp.zeros(even[0].shape, jnp.float32)]
    odd = [jnp.where(half, turned[p], turned[p + 1]) for p in range(pairs)]
    for p in range(pairs):
        total = None
        for j in range(width):
            if p + j // 2 < pairs:
                term = factor[j] * (odd if j % 2 else even)[p + j // 2]
                total = term if total is None else total + term
        done[2 * p] = total[:part]
        done[2 * p + 1] = total[part:]
        finish(2 * p + 1)
    for copy in copies:
        copy.wait()


def shape(*dims, dtype=jnp.float32):
    return jax.ShapeDtypeStruct(dims, dtype)


def spec(space):
    return pl.BlockSpec(memory_space=space)


def body(
    adjoint_eta,
    adjoint_flow,
    residual,
    sensor_cell,
    sensor_count,
    depth_class,
    speed_table,
    damping,
    profile,
    band_weight,
):
    tiles = lax.axis_size("trench")
    blocks = lax.axis_size("tblock")
    levels, rows, across = adjoint_eta.shape[1:]
    tall = rows + 2 * PAD
    params = pltpu.CompilerParams(vmem_limit_bytes=LIMIT)

    def swaps(parts, axis):
        devices = lax.axis_size(axis)
        moved = {r: lax.ppermute(parts[r], axis, [(i, i ^ r) for i in range(devices)]) for r in range(devices - 1, 0, -1)}
        return [parts[0]] + [moved[r] for r in range(1, devices)]

    own = residual[0, 0]
    slots = own.shape[2]
    chips = tiles // 2

    def meet(x, d):
        pairs = [(2 * c + 1, 2 * ((c + d) % chips)) for c in range(chips)]
        return lax.ppermute(x, "trench", pairs + [(j, i) for i, j in pairs])

    partner = meet(own, 0)
    matrix = shape(16 * (len(FIELDS) + 1), 8 * levels, dtype=jnp.bfloat16)
    w_eta, w_flow, cel, coef, factor, own, eta, flow = pl.pallas_call(
        prepare_kernel,
        out_shape=(
            matrix,
            matrix,
            shape(rows, across),
            shape(8 * STEPS, across),
            shape(band_weight.shape[0], across),
            shape(*own.shape),
            shape(*adjoint_eta.shape),
            shape(*adjoint_flow.shape),
        ),
        in_specs=[spec(pltpu.HBM)] * 8,
        out_specs=(spec(VMEM),) * 8,
        scratch_shapes=[
            VMEM((rows, across), jnp.int32),
            SMEM(speed_table.shape, jnp.float32),
            VMEM((1, levels), jnp.float32),
            VMEM((1, levels), jnp.float32),
            VMEM((1, band_weight.shape[0]), jnp.float32),
            pltpu.SemaphoreType.DMA((8,)),
        ],
        compiler_params=params,
        cost_estimate=pl.CostEstimate(flops=10**7, bytes_accessed=4 * 10**6, transcendentals=0),
        name="prepare",
    )(
        *[
            pltpu.with_memory_space_constraint(x, pltpu.HBM)
            for x in (
                depth_class, speed_table, damping[None], profile[None], band_weight[None],
                own, adjoint_eta, adjoint_flow,
            )
        ]
    )
    fields, inner, outer, *relays = pl.pallas_call(
        contract_kernel,
        out_shape=(
            shape(len(FIELDS), rows, across),
            shape(ROWS, across),
            shape(STEPS + ROWS, across),
        ) + tuple(
            shape(STEPS, 6 * slots * (2 if d <= passed_on(tiles) else 1)) for d in range(2, direct(tiles) + 1)
        ),
        in_specs=[spec(VMEM)] * 7,
        out_specs=(spec(VMEM),) * (2 + direct(tiles)),
        compiler_params=params,
        cost_estimate=pl.CostEstimate(flops=10**9, bytes_accessed=4 * 10**6, transcendentals=0),
        name="contract",
    )(eta, flow, w_eta, w_flow, cel, own, partner)
    facing_out = meet(outer, 1)
    gots = [facing_out] + [meet(relay, d) for d, relay in enumerate(relays, 2)]
    late = 2 * passed_on(tiles)

    def slot_shapes(count):
        return shape(across, 3 * slots * count, dtype=jnp.bfloat16), shape(8, 3 * slots * count, dtype=jnp.int32)

    hot, places, hot_late, places_late = pl.pallas_call(
        functools.partial(sensors_kernel, rows),
        out_shape=slot_shapes(tiles - late) + slot_shapes(late),
        in_specs=[spec(VMEM), spec(SMEM)],
        out_specs=(spec(VMEM),) * 4,
        compiler_params=params,
        cost_estimate=pl.CostEstimate(flops=10**6, bytes_accessed=2 * 10**6, transcendentals=0),
        name="sensors",
    )(sensor_cell, sensor_count)
    facing_in = meet(
        pl.pallas_call(
            functools.partial(pass_kernel, slots, passed_on(tiles)),
            out_shape=shape(STEPS * -(-passed_on(tiles) // 2) + ROWS, across),
            in_specs=[spec(VMEM), spec(pl.ANY)] + [spec(VMEM)] * len(gots),
            out_specs=spec(VMEM),
            compiler_params=params,
            name="pass",
        )(inner, places_late, *gots),
        0,
    )
    planes = pl.pallas_call(
        inject_kernel,
        out_shape=shape(STEPS * (rows + 2 * PAD), across),
        in_specs=[spec(VMEM)] * (4 + len(gots)),
        out_specs=spec(VMEM),
        compiler_params=params,
        cost_estimate=pl.CostEstimate(flops=10**8, bytes_accessed=4 * 10**6, transcendentals=0),
        name="inject",
    )(hot, places, own, partner, *gots)
    series = pl.pallas_call(
        functools.partial(advance_kernel, tiles),
        out_shape=(shape(STEPS * rows // blocks, across),) * blocks,
        in_specs=[spec(VMEM)] * 8,
        out_specs=(spec(VMEM),) * blocks,
        scratch_shapes=[
            VMEM((blocks, STEPS * rows // blocks, across), jnp.float32),
            VMEM((len(HALO), tall, across), jnp.float32),
            VMEM((tall, across), jnp.float32),
        ],
        compiler_params=params,
        name="advance",
    )(fields, cel, coef, hot_late, places_late, facing_in, facing_out, planes)
    gots = swaps(series, "tblock")
    return pl.pallas_call(
        prior_kernel,
        out_shape=shape(STEPS * blocks, rows // blocks, across),
        in_specs=[spec(VMEM)] * (blocks + 1),
        out_specs=spec(pl.ANY),
        scratch_shapes=[
            VMEM((blocks, STEPS * rows // blocks, across), jnp.float32),
            VMEM((STEPS * blocks, rows // blocks, across), jnp.float32),
            pltpu.SemaphoreType.DMA((4,)),
        ],
        compiler_params=params,
        name="prior",
    )(*reversed(gots), factor)


def solution(mesh):
    in_specs = (
        P("tblock", None, "trench", None),
        P("tblock", None, "trench", None),
        P("tblock", "trench", None, None, None),
        P(),
        P(),
        P("trench", None),
        P(),
        P(),
        P(),
        P(),
    )
    out_specs = P(None, ("trench", "tblock"), None)
    return jax.shard_map(body, mesh=mesh, in_specs=in_specs, out_specs=out_specs, check_vma=False)
```

profile of v0, /device:TPU:0, one launch (start us, length us, event | category | flops | bytes accessed | tf_op | source)
XLA Modules:
  0.0 20.5 jit_solution(5664294036949987850)
XLA Ops:
  0.0 0.5 %collective-permute-start = (f32[8,4,32]{2,1,0:T(4,128)}, f32[8,4,32]{2,1,0:T(4,128)S(1)}, u32[]{:S(2)}, u32[]{:S(2)}) collective-permute-start(f32[8,4,32]{2,1,0:T(4,128)} %bitcast.4), channel_id=1, source_target_pairs={{4,0},{12,8},{20,16},{28,24},{0,4},{8,12},{16,20},{24,28},{5,1},{1... | collective-permute-start | bytes 12296 | tf_op jit(solution)/shard_map/ppermute | solution.py:396
  0.5 1.7 %prepare.1 = (bf16[192,240]{1,0:T(8,128)(2,1)S(1)}, bf16[192,240]{1,0:T(8,128)(2,1)S(1)}, f32[16,512]{1,0:T(8,128)S(1)}, f32[32,512]{1,0:T(8,128)S(1)}, f32[8,51...) custom-call(s32[16,512]{1,0:T(8,128)} %depth.1, ...), custom_call_target="tpu_custom_call" | custom-call | flops 10000000 | bytes 4000000 | tf_op jit(solution)/shard_map/prepare/pallas_call | solution.py:400
  2.1 0.0 collective-permute-done.partner
  2.1 0.0 copy-start
  2.1 0.0 copy-start.1
  2.1 0.5 %contract.1 = (f32[11,16,512]{2,1,0:T(8,128)S(1)}, f32[17,512]{1,0:T(8,128)S(1)}, f32[21,512]{1,0:T(8,128)S(1)}, f32[4,192]{1,0:T(4,128)S(1)}) custom-call(f32[1,30,16,512]{3,2,1,0:T(8,128)S(1)} %get-tuple-element.25.eta, f32[1,30,16,512]{3,2,1,0:T(8,128)S(1)} %get-tuple-element.26.flow, bf16[192,240]{1,0:T(8,128)(2,1)S(1)} %get-tuple-element.27.w_eta, ...), custom_call_target="tpu_custom_call" | custom-call | flops 1000000000 | bytes 4000000 | tf_op jit(solution)/shard_map/contract/pallas_call | solution.py:434
  2.7 3.6 %collective-permute-start.1 = (f32[21,512]{1,0:T(8,128)S(1)}, f32[21,512]{1,0:T(8,128)S(1)}, u32[]{:S(2)}, u32[]{:S(2)}) collective-permute-start(f32[21,512]{1,0:T(8,128)S(1)} %get-tuple-element.36), channel_id=1, source_target_pairs={{4,8},{12,16},{20,24},{28,0},{8,4},{16,12},{24,20},{0,28},{5,9},{1... | collective-permute-start | bytes 129032 | tf_op jit(solution)/shard_map/ppermute | solution.py:396
  6.3 0.2 collective-permute-start.2
  6.5 0.0 copy-done
  6.5 1.1 %sensors.1 = (bf16[512,576]{1,0:T(8,128)(2,1)S(1)}, s32[8,576]{1,0:T(8,128)S(1)}, bf16[512,192]{1,0:T(8,128)(2,1)S(1)}, s32[8,192]{1,0:T(8,128)S(1)}) custom-call(s32[8,8,32]{2,1,0:T(8,128)S(1)} %copy-done, s32[8,8]{1,0:T(8,128)S(1)} %copy-done.1), custom_call_target="tpu_custom_call" | custom-call | flops 1000000 | bytes 2000000 | tf_op jit(solution)/shard_map/sensors/pallas_call | solution.py:456
  7.6 1.8 %collective-permute-done.2.refs_1_ = f32[4,192]{1,0:T(4,128)S(1)} collective-permute-done((f32[4,192]{1,0:T(4,128)S(1)}, f32[4,192]{1,0:T(4,128)S(1)}, u32[]{:S(2)}, u32[]{:S(2)}) %collective-permute-start.2) | collective-permute-done | bytes 3104 | tf_op jit(solution)/shard_map/ppermute | solution.py:396
  9.4 0.0 collective-permute-done.1.refs_0_.facing_out
  9.4 0.1 pass.1
  9.4 0.0 collective-permute-start.3
  9.5 0.5 %inject.1.planes = f32[128,512]{1,0:T(8,128)S(1)} custom-call(bf16[512,576]{1,0:T(8,128)(2,1)S(1)} %get-tuple-element.38.hot, s32[8,576]{1,0:T(8,128)S(1)} %get-tuple-element.39.places, f32[8,4,32]{2,1,0:T(4,128)S(1)} %get-tuple-element.30.own, f32[8,4,32]{2,1,0:T(4,128)S(1)} %collective-permute-done.partner, ...), custom_call_target="tpu_custom_call" | custom-call | flops 100000000 | bytes 4000000 | tf_op jit(solution)/shard_map/inject/pallas_call | solution.py:476
  10.0 0.7 %collective-permute-done.3.facing_in = f32[21,512]{1,0:T(8,128)S(1)} collective-permute-done((f32[21,512]{1,0:T(8,128)S(1)}, f32[21,512]{1,0:T(8,128)S(1)}, u32[]{:S(2)}, u32[]{:S(2)}) %collective-permute-start.3) | collective-permute-done | bytes 43040 | tf_op jit(solution)/shard_map/ppermute | solution.py:396
  10.7 0.6 %advance.1 = (f32[16,512]{1,0:T(8,128)S(1)}, f32[16,512]{1,0:T(8,128)S(1)}, f32[16,512]{1,0:T(8,128)S(1)}, f32[16,512]{1,0:T(8,128)S(1)}) custom-call(f32[11,16,512]{2,1,0:T(8,128)S(1)} %get-tuple-element.31.fields, f32[16,512]{1,0:T(8,128)S(1)} %get-tuple-element.29.cel, f32[32,512]{1,0:T(8,128)S(1)} %get-tuple-element.32.coef, ...), custom_call_target="tpu_custom_call" | custom-call | tf_op jit(solution)/shard_map/advance/pallas_call | solution.py:485
  11.3 3.7 %collective-permute-start.4 = (f32[16,512]{1,0:T(8,128)S(1)}, f32[16,512]{1,0:T(8,128)S(1)}, u32[]{:S(2)}, u32[]{:S(2)}) collective-permute-start(f32[16,512]{1,0:T(8,128)S(1)} %get-tuple-element.40), channel_id=1, source_target_pairs={{0,3},{1,2},{2,1},{3,0},{4,7},{5,6},{6,5},{7,4},{8,11},{9,10},{10,... | collective-permute-start | bytes 98312 | tf_op jit(solution)/shard_map/ppermute | solution.py:387
  15.0 0.0 collective-permute-start.5
  15.0 0.8 %collective-permute-start.6 = (f32[16,512]{1,0:T(8,128)S(1)}, f32[16,512]{1,0:T(8,128)S(1)}, u32[]{:S(2)}, u32[]{:S(2)}) collective-permute-start(f32[16,512]{1,0:T(8,128)S(1)} %get-tuple-element.42), channel_id=1, source_target_pairs={{0,1},{1,0},{2,3},{3,2},{4,5},{5,4},{6,7},{7,6},{8,9},{9,8},{10,11... | collective-permute-start | bytes 98312 | tf_op jit(solution)/shard_map/ppermute | solution.py:387
  15.8 1.3 %collective-permute-done.4.refs_0_ = f32[16,512]{1,0:T(8,128)S(1)} collective-permute-done((f32[16,512]{1,0:T(8,128)S(1)}, f32[16,512]{1,0:T(8,128)S(1)}, u32[]{:S(2)}, u32[]{:S(2)}) %collective-permute-start.4) | collective-permute-done | bytes 32800 | tf_op jit(solution)/shard_map/ppermute | solution.py:387
  17.1 2.7 %collective-permute-done.5.refs_1_ = f32[16,512]{1,0:T(8,128)S(1)} collective-permute-done((f32[16,512]{1,0:T(8,128)S(1)}, f32[16,512]{1,0:T(8,128)S(1)}, u32[]{:S(2)}, u32[]{:S(2)}) %collective-permute-start.5) | collective-permute-done | bytes 32800 | tf_op jit(solution)/shard_map/ppermute | solution.py:387
  19.8 0.0 collective-permute-done.6.refs_2_
  19.8 0.7 %prior.1 = f32[16,4,512]{2,1,0:T(4,128)} custom-call(f32[16,512]{1,0:T(8,128)S(1)} %collective-permute-done.4.refs_0_, f32[16,512]{1,0:T(8,128)S(1)} %collective-permute-done.5.refs_1_, f32[16,512]{1,0:T(8,128)S(1)} %collective-permute-done.6.refs_2_, f32[16,512]{1,0:T(8,128)S(1)} %get-tuple-element.43.refs_3_, f32[8,512]{1,0:T(8,128)S(1)} %get-tuple-element.44.refs_4_), custom_call_target="tpu_custom_call" | custom-call | tf_op jit(solution)/shard_map/prior/pallas_call | solution.py:499
  (1 shorter events, 0.0 us)
Async XLA Ops:
  0.0 2.1 %collective-permute-start = (f32[8,4,32]{2,1,0:T(4,128)}, f32[8,4,32]{2,1,0:T(4,128)S(1)}, u32[]{:S(2)}, u32[]{:S(2)}) collective-permute-start(f32[8,4,32]{2,1,0:T(4,128)} %bitcast.4), channel_id=1, source_target_pairs={{4,0},{12,8},{20,16},{28,24},{0,4},{8,12},{16,20},{24,28},{5,1},{1... | collective-permute-start | bytes 12296 | tf_op jit(solution)/shard_map/ppermute | solution.py:396
  2.1 4.4 %copy-start = (s32[8,8,32]{2,1,0:T(8,128)S(1)}, s32[8,8,32]{2,1,0:T(8,128)}, u32[]{:S(2)}) copy-start(s32[8,8,32]{2,1,0:T(8,128)} %cells.1) | copy-start | bytes 24580
  2.1 4.4 %copy-start.1 = (s32[8,8]{1,0:T(8,128)S(1)}, s32[8,8]{1,0:T(8,128)}, u32[]{:S(2)}) copy-start(s32[8,8]{1,0:T(8,128)} %count.1) | copy-start | bytes 772
  2.7 6.7 %collective-permute-start.1 = (f32[21,512]{1,0:T(8,128)S(1)}, f32[21,512]{1,0:T(8,128)S(1)}, u32[]{:S(2)}, u32[]{:S(2)}) collective-permute-start(f32[21,512]{1,0:T(8,128)S(1)} %get-tuple-element.36), channel_id=1, source_target_pairs={{4,8},{12,16},{20,24},{28,0},{8,4},{16,12},{24,20},{0,28},{5,9},{1... | collective-permute-start | bytes 129032 | tf_op jit(solution)/shard_map/ppermute | solution.py:396
  6.3 3.0 %collective-permute-start.2 = (f32[4,192]{1,0:T(4,128)S(1)}, f32[4,192]{1,0:T(4,128)S(1)}, u32[]{:S(2)}, u32[]{:S(2)}) collective-permute-start(f32[4,192]{1,0:T(4,128)S(1)} %get-tuple-element.37), channel_id=1, source_target_pairs={{4,16},{12,24},{20,0},{28,8},{16,4},{24,12},{0,20},{8,28},{5,17},{... | collective-permute-start | bytes 9224 | tf_op jit(solution)/shard_map/ppermute | solution.py:396
  9.4 1.2 %collective-permute-start.3 = (f32[21,512]{1,0:T(8,128)S(1)}, f32[21,512]{1,0:T(8,128)S(1)}, u32[]{:S(2)}, u32[]{:S(2)}) collective-permute-start(f32[21,512]{1,0:T(8,128)S(1)} %pass.1), channel_id=1, source_target_pairs={{4,0},{12,8},{20,16},{28,24},{0,4},{8,12},{16,20},{24,28},{5,1},{1... | collective-permute-start | bytes 129032 | tf_op jit(solution)/shard_map/ppermute | solution.py:396
  11.3 5.8 %collective-permute-start.4 = (f32[16,512]{1,0:T(8,128)S(1)}, f32[16,512]{1,0:T(8,128)S(1)}, u32[]{:S(2)}, u32[]{:S(2)}) collective-permute-start(f32[16,512]{1,0:T(8,128)S(1)} %get-tuple-element.40), channel_id=1, source_target_pairs={{0,3},{1,2},{2,1},{3,0},{4,7},{5,6},{6,5},{7,4},{8,11},{9,10},{10,... | collective-permute-start | bytes 98312 | tf_op jit(solution)/shard_map/ppermute | solution.py:387
  15.0 4.8 %collective-permute-start.5 = (f32[16,512]{1,0:T(8,128)S(1)}, f32[16,512]{1,0:T(8,128)S(1)}, u32[]{:S(2)}, u32[]{:S(2)}) collective-permute-start(f32[16,512]{1,0:T(8,128)S(1)} %get-tuple-element.41), channel_id=1, source_target_pairs={{0,2},{1,3},{2,0},{3,1},{4,6},{5,7},{6,4},{7,5},{8,10},{9,11},{10,... | collective-permute-start | bytes 98312 | tf_op jit(solution)/shard_map/ppermute | solution.py:387
  15.0 4.8 %collective-permute-start.6 = (f32[16,512]{1,0:T(8,128)S(1)}, f32[16,512]{1,0:T(8,128)S(1)}, u32[]{:S(2)}, u32[]{:S(2)}) collective-permute-start(f32[16,512]{1,0:T(8,128)S(1)} %get-tuple-element.42), channel_id=1, source_target_pairs={{0,1},{1,0},{2,3},{3,2},{4,5},{5,4},{6,7},{7,6},{8,9},{9,8},{10,11... | collective-permute-start | bytes 98312 | tf_op jit(solution)/shard_map/ppermute | solution.py:387
where the time goes:
time: 20.7 us; the launch traced here: 20.5 us
  starting transfers between devices  8.72 us (42%)
  waiting for transfers between devices  6.54 us (32%)
  Pallas kernels  5.19 us (25%)
    ppermute x3, starting transfers between devices, swaps(): lax.ppermute(parts[r], axis, [(i, i ^ r) for i in range(devices)])  4.45 us
    ppermute x4, starting transfers between devices, meet(): return lax.ppermute(x, 'trench', pairs + [(j, i) for i, j in pairs])  4.27 us
    ppermute x3, waiting for transfers between devices, swaps(): lax.ppermute(parts[r], axis, [(i, i ^ r) for i in range(devices)])  4.02 us
    ppermute x4, waiting for transfers between devices, meet(): return lax.ppermute(x, 'trench', pairs + [(j, i) for i, j in pairs])  2.51 us
    pallas_call x1, Pallas kernels, body(): pl.pallas_call(prepare_kernel, out_shape=(matrix, matrix, shape(rows, acr...  1.65 us
    pallas_call x1, Pallas kernels, body(): pl.pallas_call(functools.partial(sensors_kernel, rows), out_shape=slot_sh...  1.07 us
    pallas_call x1, Pallas kernels, body(): pl.pallas_call(prior_kernel, out_shape=shape(STEPS * blocks, rows // bloc...  0.74 us
    pallas_call x1, Pallas kernels, body(): pl.pallas_call(functools.partial(advance_kernel, tiles), out_shape=(shape...  0.62 us
  transfers between devices with their start and end apart: 7, of which 4 were waited for; matrix products, arithmetic and copies ran while one was open for 0% of the time, Pallas kernels for 16%

commit v1 on v0

--- a/solution.py
+++ b/solution.py
@@ -18,11 +18,17 @@
 SHIFT = 1.2
 
 FIELDS = [(4, 4), (4, 3), (4, 2), (3, 2), (4, 1), (3, 1), (2, 1), (4, 0), (3, 0), (2, 0), (1, 0)]
-HALO = [4, 3, 2, 2, 1, 1, 1]
-HALO_AT = [0, 4, 7, 9, 11, 12, 13]
-CEL_AT = 14
+TRACED = [(4, 4), (4, 3), (3, 2), (2, 1), (4, 2), (3, 1), (4, 1)]
+CEL_AT = len(TRACED)
 CEL_HALO = 3
-ROWS = 17
+ROWS = CEL_AT + CEL_HALO
+
+
+def beside(z):
+    across = z.shape[1]
+    lane = lax.broadcasted_iota(jnp.int32, z.shape, 1)
+    left = jnp.where(lane == 0, 0.0, pltpu.roll(z, 1, 1))
+    return left + jnp.where(lane == across - 1, 0.0, pltpu.roll(z, across - 1, 1))
 
 
 def split(x):
@@ -132,10 +138,25 @@
         out = relays[d - 2] if d > 1 else outer
         out[0:STEPS, :] = widen(values, out.shape[1])
 
+    speed = cel[...]
+    row = lax.broadcasted_iota(jnp.int32, (rows, across), 0)
+
+    def horizontal(z):
+        around = jnp.where(row == 0, 0.0, pltpu.roll(z, 1, 0)) + jnp.where(row == rows - 1, 0.0, pltpu.roll(z, rows - 1, 0))
+        return speed * (around + beside(z) - 4.0 * z) + SHIFT * z
+
+    operand = {(STEPS, STEPS): fields[0]}
+    base = horizontal(fields[0])
+    for n in range(2, STEPS + 1):
+        z = base
+        for k in range(n - 1, 0, -1):
+            operand[n, k] = z + fields[FIELDS.index((n, k))]
+            if k > 1:
+                z = horizontal(operand[n, k])
+
     def edge(out, at, last):
-        for f, width in enumerate(HALO):
-            start = rows - width if last else 0
-            out[at + HALO_AT[f] : at + HALO_AT[f] + width, :] = fields[f, start : start + width, :]
+        for f, key in enumerate(TRACED):
+            out[at + f : at + f + 1, :] = operand[key][rows - 1 : rows] if last else operand[key][0:1]
         start = rows - CEL_HALO if last else 0
         out[at + CEL_AT : at + CEL_AT + CEL_HALO, :] = cel[start : start + CEL_HALO, :]
 
@@ -244,7 +265,7 @@
 
 
 def advance_kernel(tiles, fields, cel, coef, hot, places, facing_in, facing_out, planes, *refs):
-    outs, (stage, ext, cel_ext) = refs[:-3], refs[-3:]
+    outs, (stage, cel_ext) = refs[:-2], refs[-2:]
     blocks = len(outs)
     me = lax.axis_index("trench")
     rows, across = cel.shape
@@ -264,31 +285,24 @@
     all_planes = planes[...] + planes_of(jnp.concatenate(late, axis=1), hot, places, tall)
     inject = [all_planes[tall * t : tall * t + tall] for t in range(STEPS)]
 
-    def extend(store, own, at, width):
-        store(0, PAD, jnp.zeros((PAD, across), jnp.float32))
-        store(PAD + rows, tall, jnp.zeros((PAD, across), jnp.float32))
-        store(PAD, PAD + rows, own)
-        store(PAD - width, PAD, before[at : at + width])
-        store(PAD + rows, PAD + rows + width, after[at : at + width])
-
-    for f, width in enumerate(HALO):
-        def store(a, b, value, f=f):
-            ext[f, a:b, :] = value
-        extend(store, fields[f], HALO_AT[f], width)
-
-    def store_cel(a, b, value):
-        cel_ext[a:b, :] = value
-    extend(store_cel, cel[...], CEL_AT, CEL_HALO)
-
-    lane = lax.broadcasted_iota(jnp.int32, (tall, across), 1)
-    first = lane == 0
-    last = lane == across - 1
+    cel_ext[...] = jnp.zeros((tall, across), jnp.float32)
+    cel_ext[PAD - CEL_HALO : PAD, :] = before[CEL_AT:]
+    cel_ext[PAD : PAD + rows, :] = cel[...]
+    cel_ext[PAD + rows : PAD + rows + CEL_HALO, :] = after[CEL_AT:]
+
+
+    row = lax.broadcasted_iota(jnp.int32, (tall, across), 0)
     speed = cel_ext[...]
-
-    def horizontal(z):
-        around = pltpu.roll(z, 1, 0) + pltpu.roll(z, tall - 1, 0)
-        around += jnp.where(first, 0.0, pltpu.roll(z, 1, 1))
-        around += jnp.where(last, 0.0, pltpu.roll(z, across - 1, 1))
+    margin = jnp.zeros((PAD, across), jnp.float32)
+
+    def own(n, k):
+        return jnp.concatenate([margin, fields[FIELDS.index((n, k))], margin], axis=0)
+
+    def horizontal(z, n, k):
+        at = TRACED.index((n, k))
+        facing = jnp.where(row == PAD + rows - 1, after[at : at + 1], 0.0)
+        facing = jnp.where(row == PAD, before[at : at + 1], facing)
+        around = pltpu.roll(z, 1, 0) + pltpu.roll(z, tall - 1, 0) + facing + beside(z)
         return speed * (around - 4.0 * z) + SHIFT * z
 
     def injected(n, k, a, b):
@@ -299,15 +313,15 @@
             total = term if total is None else total + term
         return total
 
-    base = horizontal(ext[0])
+    base = horizontal(own(STEPS, STEPS), STEPS, STEPS)
     for n in range(1, STEPS + 1):
         z = base
         for k in range(n - 1, 0, -1):
-            z = horizontal(z + ext[FIELDS.index((n, k))] + injected(n, k, 0, tall))
-        own = z[PAD : PAD + rows] + fields[FIELDS.index((n, 0))] + injected(n, 0, PAD, PAD + rows)
+            z = horizontal(z + own(n, k) + injected(n, k, 0, tall), n, k)
+        series = z[PAD : PAD + rows] + fields[FIELDS.index((n, 0))] + injected(n, 0, PAD, PAD + rows)
         t = STEPS - n
         for b in range(blocks):
-            stage[b, part * t : part * t + part, :] = own[part * b : part * b + part]
+            stage[b, part * t : part * t + part, :] = series[part * b : part * b + part]
     block = lax.axis_index("tblock")
     for r, out in enumerate(outs):
         out[...] = stage[block ^ r]
@@ -489,7 +503,6 @@
         out_specs=(spec(VMEM),) * blocks,
         scratch_shapes=[
             VMEM((blocks, STEPS * rows // blocks, across), jnp.float32),
-            VMEM((len(HALO), tall, across), jnp.float32),
             VMEM((tall, across), jnp.float32),
         ],
         compiler_params=params,

time: 20.7 us -> 20.9 us (level)
  Pallas kernels: 5.19 us -> 5.42 us
    pallas_call x1, Pallas kernels: 0.54 us -> 0.79 us  [body(): pl.pallas_call(contract_kernel, out_shape=(shape(len(FIELDS), rows, acros...]
  transfers between devices with their start and end apart: 7 -> 7, of which waited for: 4 -> 4; matrix products, arithmetic and copies ran while one was open for 0% -> 0% of each run, Pallas kernels for 16% -> 15%
where the time goes in v1:
time: 20.9 us; the launch traced here: 20.7 us
  starting transfers between devices  8.71 us (42%)
  waiting for transfers between devices  6.52 us (31%)
  Pallas kernels  5.42 us (26%)
    ppermute x3, starting transfers between devices, swaps(): lax.ppermute(parts[r], axis, [(i, i ^ r) for i in range(devices)])  4.45 us
    ppermute x4, starting transfers between devices, meet(): return lax.ppermute(x, 'trench', pairs + [(j, i) for i, j in pairs])  4.26 us
    ppermute x3, waiting for transfers between devices, swaps(): lax.ppermute(parts[r], axis, [(i, i ^ r) for i in range(devices)])  4.02 us
    ppermute x4, waiting for transfers between devices, meet(): return lax.ppermute(x, 'trench', pairs + [(j, i) for i, j in pairs])  2.5 us
    pallas_call x1, Pallas kernels, body(): pl.pallas_call(prepare_kernel, out_shape=(matrix, matrix, shape(rows, acr...  1.65 us
    pallas_call x1, Pallas kernels, body(): pl.pallas_call(functools.partial(sensors_kernel, rows), out_shape=slot_sh...  1.07 us
    pallas_call x1, Pallas kernels, body(): pl.pallas_call(contract_kernel, out_shape=(shape(len(FIELDS), rows, acros...  0.79 us
    pallas_call x1, Pallas kernels, body(): pl.pallas_call(prior_kernel, out_shape=shape(STEPS * blocks, rows // bloc...  0.74 us
  transfers between devices with their start and end apart: 7, of which 4 were waited for; matrix products, arithmetic and copies ran while one was open for 0% of the time, Pallas kernels for 15%

profile of v1, /device:TPU:0, one launch (start us, length us, event | category | flops | bytes accessed | tf_op | source)
XLA Modules:
  0.0 20.7 jit_solution(18177501689296990161)
XLA Ops:
  0.0 0.5 %collective-permute-start = (f32[8,4,32]{2,1,0:T(4,128)}, f32[8,4,32]{2,1,0:T(4,128)S(1)}, u32[]{:S(2)}, u32[]{:S(2)}) collective-permute-start(f32[8,4,32]{2,1,0:T(4,128)} %bitcast.4), channel_id=1, source_target_pairs={{4,0},{12,8},{20,16},{28,24},{0,4},{8,12},{16,20},{24,28},{5,1},{1... | collective-permute-start | bytes 12296 | tf_op jit(solution)/shard_map/ppermute | solution.py:410
  0.5 1.7 %prepare.1 = (bf16[192,240]{1,0:T(8,128)(2,1)S(1)}, bf16[192,240]{1,0:T(8,128)(2,1)S(1)}, f32[16,512]{1,0:T(8,128)S(1)}, f32[32,512]{1,0:T(8,128)S(1)}, f32[8,51...) custom-call(s32[16,512]{1,0:T(8,128)} %depth.1, ...), custom_call_target="tpu_custom_call" | custom-call | flops 10000000 | bytes 4000000 | tf_op jit(solution)/shard_map/prepare/pallas_call | solution.py:414
  2.1 0.0 collective-permute-done.partner
  2.1 0.0 copy-start
  2.1 0.0 copy-start.1
  2.1 0.8 %contract.1 = (f32[11,16,512]{2,1,0:T(8,128)S(1)}, f32[10,512]{1,0:T(8,128)S(1)}, f32[14,512]{1,0:T(8,128)S(1)}, f32[4,192]{1,0:T(4,128)S(1)}) custom-call(f32[1,30,16,512]{3,2,1,0:T(8,128)S(1)} %get-tuple-element.25.eta, f32[1,30,16,512]{3,2,1,0:T(8,128)S(1)} %get-tuple-element.26.flow, bf16[192,240]{1,0:T(8,128)(2,1)S(1)} %get-tuple-element.27.w_eta, ...), custom_call_target="tpu_custom_call" | custom-call | flops 1000000000 | bytes 4000000 | tf_op jit(solution)/shard_map/contract/pallas_call | solution.py:448
  2.9 3.6 %collective-permute-start.1 = (f32[14,512]{1,0:T(8,128)S(1)}, f32[14,512]{1,0:T(8,128)S(1)}, u32[]{:S(2)}, u32[]{:S(2)}) collective-permute-start(f32[14,512]{1,0:T(8,128)S(1)} %get-tuple-element.36), channel_id=1, source_target_pairs={{4,8},{12,16},{20,24},{28,0},{8,4},{16,12},{24,20},{0,28},{5,9},{1... | collective-permute-start | bytes 86024 | tf_op jit(solution)/shard_map/ppermute | solution.py:410
  6.6 0.2 collective-permute-start.2
  6.7 0.0 copy-done
  6.8 1.1 %sensors.1 = (bf16[512,576]{1,0:T(8,128)(2,1)S(1)}, s32[8,576]{1,0:T(8,128)S(1)}, bf16[512,192]{1,0:T(8,128)(2,1)S(1)}, s32[8,192]{1,0:T(8,128)S(1)}) custom-call(s32[8,8,32]{2,1,0:T(8,128)S(1)} %copy-done, s32[8,8]{1,0:T(8,128)S(1)} %copy-done.1), custom_call_target="tpu_custom_call" | custom-call | flops 1000000 | bytes 2000000 | tf_op jit(solution)/shard_map/sensors/pallas_call | solution.py:470
  7.8 1.8 %collective-permute-done.2.refs_1_ = f32[4,192]{1,0:T(4,128)S(1)} collective-permute-done((f32[4,192]{1,0:T(4,128)S(1)}, f32[4,192]{1,0:T(4,128)S(1)}, u32[]{:S(2)}, u32[]{:S(2)}) %collective-permute-start.2) | collective-permute-done | bytes 3104 | tf_op jit(solution)/shard_map/ppermute | solution.py:410
  9.6 0.0 collective-permute-done.1.refs_0_.facing_out
  9.6 0.1 pass.1
  9.7 0.0 collective-permute-start.3
  9.7 0.5 %inject.1.planes = f32[128,512]{1,0:T(8,128)S(1)} custom-call(bf16[512,576]{1,0:T(8,128)(2,1)S(1)} %get-tuple-element.38.hot, s32[8,576]{1,0:T(8,128)S(1)} %get-tuple-element.39.places, f32[8,4,32]{2,1,0:T(4,128)S(1)} %get-tuple-element.30.own, f32[8,4,32]{2,1,0:T(4,128)S(1)} %collective-permute-done.partner, ...), custom_call_target="tpu_custom_call" | custom-call | flops 100000000 | bytes 4000000 | tf_op jit(solution)/shard_map/inject/pallas_call | solution.py:490
  10.2 0.7 %collective-permute-done.3.facing_in = f32[14,512]{1,0:T(8,128)S(1)} collective-permute-done((f32[14,512]{1,0:T(8,128)S(1)}, f32[14,512]{1,0:T(8,128)S(1)}, u32[]{:S(2)}, u32[]{:S(2)}) %collective-permute-start.3) | collective-permute-done | bytes 28704 | tf_op jit(solution)/shard_map/ppermute | solution.py:410
  10.9 0.6 %advance.1 = (f32[16,512]{1,0:T(8,128)S(1)}, f32[16,512]{1,0:T(8,128)S(1)}, f32[16,512]{1,0:T(8,128)S(1)}, f32[16,512]{1,0:T(8,128)S(1)}) custom-call(f32[11,16,512]{2,1,0:T(8,128)S(1)} %get-tuple-element.31.fields, f32[16,512]{1,0:T(8,128)S(1)} %get-tuple-element.29.cel, f32[32,512]{1,0:T(8,128)S(1)} %get-tuple-element.32.coef, ...), custom_call_target="tpu_custom_call" | custom-call | tf_op jit(solution)/shard_map/advance/pallas_call | solution.py:499
  11.5 3.7 %collective-permute-start.4 = (f32[16,512]{1,0:T(8,128)S(1)}, f32[16,512]{1,0:T(8,128)S(1)}, u32[]{:S(2)}, u32[]{:S(2)}) collective-permute-start(f32[16,512]{1,0:T(8,128)S(1)} %get-tuple-element.40), channel_id=1, source_target_pairs={{0,3},{1,2},{2,1},{3,0},{4,7},{5,6},{6,5},{7,4},{8,11},{9,10},{10,... | collective-permute-start | bytes 98312 | tf_op jit(solution)/shard_map/ppermute | solution.py:401
  15.2 0.0 collective-permute-start.5
  15.2 0.8 %collective-permute-start.6 = (f32[16,512]{1,0:T(8,128)S(1)}, f32[16,512]{1,0:T(8,128)S(1)}, u32[]{:S(2)}, u32[]{:S(2)}) collective-permute-start(f32[16,512]{1,0:T(8,128)S(1)} %get-tuple-element.42), channel_id=1, source_target_pairs={{0,1},{1,0},{2,3},{3,2},{4,5},{5,4},{6,7},{7,6},{8,9},{9,8},{10,11... | collective-permute-start | bytes 98312 | tf_op jit(solution)/shard_map/ppermute | solution.py:401
  16.0 1.3 %collective-permute-done.4.refs_0_ = f32[16,512]{1,0:T(8,128)S(1)} collective-permute-done((f32[16,512]{1,0:T(8,128)S(1)}, f32[16,512]{1,0:T(8,128)S(1)}, u32[]{:S(2)}, u32[]{:S(2)}) %collective-permute-start.4) | collective-permute-done | bytes 32800 | tf_op jit(solution)/shard_map/ppermute | solution.py:401
  17.3 2.7 %collective-permute-done.5.refs_1_ = f32[16,512]{1,0:T(8,128)S(1)} collective-permute-done((f32[16,512]{1,0:T(8,128)S(1)}, f32[16,512]{1,0:T(8,128)S(1)}, u32[]{:S(2)}, u32[]{:S(2)}) %collective-permute-start.5) | collective-permute-done | bytes 32800 | tf_op jit(solution)/shard_map/ppermute | solution.py:401
  20.0 0.0 collective-permute-done.6.refs_2_
  20.0 0.7 %prior.1 = f32[16,4,512]{2,1,0:T(4,128)} custom-call(f32[16,512]{1,0:T(8,128)S(1)} %collective-permute-done.4.refs_0_, f32[16,512]{1,0:T(8,128)S(1)} %collective-permute-done.5.refs_1_, f32[16,512]{1,0:T(8,128)S(1)} %collective-permute-done.6.refs_2_, f32[16,512]{1,0:T(8,128)S(1)} %get-tuple-element.43.refs_3_, f32[8,512]{1,0:T(8,128)S(1)} %get-tuple-element.44.refs_4_), custom_call_target="tpu_custom_call" | custom-call | tf_op jit(solution)/shard_map/prior/pallas_call | solution.py:512
  (1 shorter events, 0.0 us)
Async XLA Ops:
  0.0 2.1 %collective-permute-start = (f32[8,4,32]{2,1,0:T(4,128)}, f32[8,4,32]{2,1,0:T(4,128)S(1)}, u32[]{:S(2)}, u32[]{:S(2)}) collective-permute-start(f32[8,4,32]{2,1,0:T(4,128)} %bitcast.4), channel_id=1, source_target_pairs={{4,0},{12,8},{20,16},{28,24},{0,4},{8,12},{16,20},{24,28},{5,1},{1... | collective-permute-start | bytes 12296 | tf_op jit(solution)/shard_map/ppermute | solution.py:410
  2.1 4.6 %copy-start = (s32[8,8,32]{2,1,0:T(8,128)S(1)}, s32[8,8,32]{2,1,0:T(8,128)}, u32[]{:S(2)}) copy-start(s32[8,8,32]{2,1,0:T(8,128)} %cells.1) | copy-start | bytes 24580
  2.1 4.6 %copy-start.1 = (s32[8,8]{1,0:T(8,128)S(1)}, s32[8,8]{1,0:T(8,128)}, u32[]{:S(2)}) copy-start(s32[8,8]{1,0:T(8,128)} %count.1) | copy-start | bytes 772
  2.9 6.7 %collective-permute-start.1 = (f32[14,512]{1,0:T(8,128)S(1)}, f32[14,512]{1,0:T(8,128)S(1)}, u32[]{:S(2)}, u32[]{:S(2)}) collective-permute-start(f32[14,512]{1,0:T(8,128)S(1)} %get-tuple-element.36), channel_id=1, source_target_pairs={{4,8},{12,16},{20,24},{28,0},{8,4},{16,12},{24,20},{0,28},{5,9},{1... | collective-permute-start | bytes 86024 | tf_op jit(solution)/shard_map/ppermute | solution.py:410
  6.6 3.0 %collective-permute-start.2 = (f32[4,192]{1,0:T(4,128)S(1)}, f32[4,192]{1,0:T(4,128)S(1)}, u32[]{:S(2)}, u32[]{:S(2)}) collective-permute-start(f32[4,192]{1,0:T(4,128)S(1)} %get-tuple-element.37), channel_id=1, source_target_pairs={{4,16},{12,24},{20,0},{28,8},{16,4},{24,12},{0,20},{8,28},{5,17},{... | collective-permute-start | bytes 9224 | tf_op jit(solution)/shard_map/ppermute | solution.py:410
  9.7 1.2 %collective-permute-start.3 = (f32[14,512]{1,0:T(8,128)S(1)}, f32[14,512]{1,0:T(8,128)S(1)}, u32[]{:S(2)}, u32[]{:S(2)}) collective-permute-start(f32[14,512]{1,0:T(8,128)S(1)} %pass.1), channel_id=1, source_target_pairs={{4,0},{12,8},{20,16},{28,24},{0,4},{8,12},{16,20},{24,28},{5,1},{1... | collective-permute-start | bytes 86024 | tf_op jit(solution)/shard_map/ppermute | solution.py:410
  11.5 5.8 %collective-permute-start.4 = (f32[16,512]{1,0:T(8,128)S(1)}, f32[16,512]{1,0:T(8,128)S(1)}, u32[]{:S(2)}, u32[]{:S(2)}) collective-permute-start(f32[16,512]{1,0:T(8,128)S(1)} %get-tuple-element.40), channel_id=1, source_target_pairs={{0,3},{1,2},{2,1},{3,0},{4,7},{5,6},{6,5},{7,4},{8,11},{9,10},{10,... | collective-permute-start | bytes 98312 | tf_op jit(solution)/shard_map/ppermute | solution.py:401
  15.2 4.8 %collective-permute-start.5 = (f32[16,512]{1,0:T(8,128)S(1)}, f32[16,512]{1,0:T(8,128)S(1)}, u32[]{:S(2)}, u32[]{:S(2)}) collective-permute-start(f32[16,512]{1,0:T(8,128)S(1)} %get-tuple-element.41), channel_id=1, source_target_pairs={{0,2},{1,3},{2,0},{3,1},{4,6},{5,7},{6,4},{7,5},{8,10},{9,11},{10,... | collective-permute-start | bytes 98312 | tf_op jit(solution)/shard_map/ppermute | solution.py:401
  15.2 4.8 %collective-permute-start.6 = (f32[16,512]{1,0:T(8,128)S(1)}, f32[16,512]{1,0:T(8,128)S(1)}, u32[]{:S(2)}, u32[]{:S(2)}) collective-permute-start(f32[16,512]{1,0:T(8,128)S(1)} %get-tuple-element.42), channel_id=1, source_target_pairs={{0,1},{1,0},{2,3},{3,2},{4,5},{5,4},{6,7},{7,6},{8,9},{9,8},{10,11... | collective-permute-start | bytes 98312 | tf_op jit(solution)/shard_map/ppermute | solution.py:401

commit v2 on v0

--- a/solution.py
+++ b/solution.py
@@ -124,13 +124,8 @@
 
     me = lax.axis_index("trench")
     tiles = own.shape[0]
-    for d in range(1, len(relays) + 2):
-        target = met(me, d, tiles)
-        values = [both_rows(target, own, partner)]
-        if d <= passed_on(tiles):
-            values.append(both_rows(target ^ 1, own, partner))
-        out = relays[d - 2] if d > 1 else outer
-        out[0:STEPS, :] = widen(values, out.shape[1])
+    for d, out in enumerate((outer, *relays), 1):
+        out[0:STEPS, :] = widen([both_rows(met(me, d, tiles), own, partner)], out.shape[1])
 
     def edge(out, at, last):
         for f, width in enumerate(HALO):
@@ -156,22 +151,9 @@
     return jnp.where(d == 0, me, 2 * chip + 1 - odd)
 
 
-def direct(tiles):
-    return tiles // 4
-
-
-def passed_on(tiles):
-    return tiles // 2 - 1 - direct(tiles)
-
-
 def sources(me, tiles):
-    near = [met(me, d, tiles) ^ core for d in range(direct(tiles) + 1) for core in range(2)]
-    far = [met(me ^ 1, d, tiles) ^ core for d in range(1, passed_on(tiles) + 1) for core in range(2)]
-    return near, far
-
-
-def packed(q):
-    return STEPS * (q // 2), 256 * (q % 2)
+    listed = [met(me, d, tiles) ^ core for d in range(tiles // 2) for core in range(2)]
+    return listed[:-2], listed[-2:]
 
 
 def widen(values, lanes):
@@ -188,17 +170,6 @@
 
 def both_rows(owner, own, partner):
     return jnp.concatenate([residual_rows(owner, own), residual_rows(owner, partner)], axis=1)
-
-
-def pass_kernel(slots, count, inner, after, *refs):
-    gots, out = refs[:-1], refs[-1]
-    per = 6 * slots
-    top = out.shape[0] - ROWS
-    out[0:top, :] = jnp.zeros((top, out.shape[1]), jnp.float32)
-    for q in range(count):
-        row, lane = packed(q)
-        out[row : row + STEPS, lane : lane + 256] = widen([gots[q][0:STEPS, per : 2 * per]], 256)
-    out[top:, :] = inner[...]
 
 
 def sensors_kernel(rows, cells, count, hot_early, places_early, hot_late, places_late):
@@ -243,7 +214,7 @@
     planes[...] = planes_of(jnp.concatenate(values, axis=1), hot, places, planes.shape[0] // STEPS)
 
 
-def advance_kernel(tiles, fields, cel, coef, hot, places, facing_in, facing_out, planes, *refs):
+def advance_kernel(tiles, fields, cel, coef, hot, places, facing_in, facing_out, last, planes, *refs):
     outs, (stage, ext, cel_ext) = refs[:-3], refs[-3:]
     blocks = len(outs)
     me = lax.axis_index("trench")
@@ -252,16 +223,12 @@
     part = rows // blocks
     odd = me % 2 == 1
     facing = me // 2 + jnp.where(odd, 1, -1)
-    top = facing_in.shape[0] - ROWS
-    inner = facing_in[top:, :]
+    inner = facing_in[...]
     outer = jnp.where((facing >= 0) & (facing < tiles // 2), facing_out[STEPS:, :], 0.0)
     before = jnp.where(odd, inner, outer)
     after = jnp.where(odd, outer, inner)
 
-    count = passed_on(tiles)
-    per = hot.shape[1] // count
-    late = [facing_in[row : row + STEPS, at : at + per] for row, at in map(packed, range(count))]
-    all_planes = planes[...] + planes_of(jnp.concatenate(late, axis=1), hot, places, tall)
+    all_planes = planes[...] + planes_of(last[0:STEPS, 0 : hot.shape[1]], hot, places, tall)
     inject = [all_planes[tall * t : tall * t + tall] for t in range(STEPS)]
 
     def extend(store, own, at, width):
@@ -437,55 +404,42 @@
             shape(len(FIELDS), rows, across),
             shape(ROWS, across),
             shape(STEPS + ROWS, across),
-        ) + tuple(
-            shape(STEPS, 6 * slots * (2 if d <= passed_on(tiles) else 1)) for d in range(2, direct(tiles) + 1)
-        ),
+        ) + (shape(STEPS, 6 * slots),) * (chips - 2),
         in_specs=[spec(VMEM)] * 7,
-        out_specs=(spec(VMEM),) * (2 + direct(tiles)),
+        out_specs=(spec(VMEM),) * (1 + chips),
         compiler_params=params,
         cost_estimate=pl.CostEstimate(flops=10**9, bytes_accessed=4 * 10**6, transcendentals=0),
         name="contract",
     )(eta, flow, w_eta, w_flow, cel, own, partner)
     facing_out = meet(outer, 1)
     gots = [facing_out] + [meet(relay, d) for d, relay in enumerate(relays, 2)]
-    late = 2 * passed_on(tiles)
+    facing_in = meet(inner, 0)
 
     def slot_shapes(count):
         return shape(across, 3 * slots * count, dtype=jnp.bfloat16), shape(8, 3 * slots * count, dtype=jnp.int32)
 
     hot, places, hot_late, places_late = pl.pallas_call(
         functools.partial(sensors_kernel, rows),
-        out_shape=slot_shapes(tiles - late) + slot_shapes(late),
+        out_shape=slot_shapes(tiles - 2) + slot_shapes(2),
         in_specs=[spec(VMEM), spec(SMEM)],
         out_specs=(spec(VMEM),) * 4,
         compiler_params=params,
         cost_estimate=pl.CostEstimate(flops=10**6, bytes_accessed=2 * 10**6, transcendentals=0),
         name="sensors",
     )(sensor_cell, sensor_count)
-    facing_in = meet(
-        pl.pallas_call(
-            functools.partial(pass_kernel, slots, passed_on(tiles)),
-            out_shape=shape(STEPS * -(-passed_on(tiles) // 2) + ROWS, across),
-            in_specs=[spec(VMEM), spec(pl.ANY)] + [spec(VMEM)] * len(gots),
-            out_specs=spec(VMEM),
-            compiler_params=params,
-            name="pass",
-        )(inner, places_late, *gots),
-        0,
-    )
     planes = pl.pallas_call(
         inject_kernel,
         out_shape=shape(STEPS * (rows + 2 * PAD), across),
-        in_specs=[spec(VMEM)] * (4 + len(gots)),
+        in_specs=[spec(VMEM)] * (3 + len(gots)),
         out_specs=spec(VMEM),
         compiler_params=params,
-        cost_estimate=pl.CostEstimate(flops=10**8, bytes_accessed=4 * 10**6, transcendentals=0),
+        cost_estimate=pl.CostEstimate(flops=1000, bytes_accessed=1000, transcendentals=0),
         name="inject",
-    )(hot, places, own, partner, *gots)
+    )(hot, places, own, partner, *gots[:-1])
     series = pl.pallas_call(
         functools.partial(advance_kernel, tiles),
         out_shape=(shape(STEPS * rows // blocks, across),) * blocks,
-        in_specs=[spec(VMEM)] * 8,
+        in_specs=[spec(VMEM)] * 9,
         out_specs=(spec(VMEM),) * blocks,
         scratch_shapes=[
             VMEM((blocks, STEPS * rows // blocks, across), jnp.float32),
@@ -494,7 +448,7 @@
         ],
         compiler_params=params,
         name="advance",
-    )(fields, cel, coef, hot_late, places_late, facing_in, facing_out, planes)
+    )(fields, cel, coef, hot_late, places_late, facing_in, facing_out, gots[-1], planes)
     gots = swaps(series, "tblock")
     return pl.pallas_call(
         prior_kernel,

time: 20.7 us -> 20.1 us (0.971)
  waiting for transfers between devices: 6.54 us -> 5.34 us
  starting transfers between devices: 8.72 us -> 9.35 us
    ppermute x4 -> x5, waiting for transfers between devices: 2.51 us -> 1.25 us  [meet(): return lax.ppermute(x, 'trench', pairs + [(j, i) for i, j in pairs])]
    ppermute x4 -> x5, starting transfers between devices: 4.27 us -> 4.9 us  [meet(): return lax.ppermute(x, 'trench', pairs + [(j, i) for i, j in pairs])]
  transfers between devices with their start and end apart: 7 -> 8, of which waited for: 4 -> 4; matrix products, arithmetic and copies ran while one was open for 0% -> 0% of each run, Pallas kernels for 16% -> 16%
where the time goes in v2:
time: 20.1 us; the launch traced here: 19.9 us
  starting transfers between devices  9.35 us (47%)
  waiting for transfers between devices  5.34 us (27%)
  Pallas kernels  5.13 us (26%)
    ppermute x5, starting transfers between devices, meet(): return lax.ppermute(x, 'trench', pairs + [(j, i) for i, j in pairs])  4.9 us
    ppermute x3, starting transfers between devices, swaps(): lax.ppermute(parts[r], axis, [(i, i ^ r) for i in range(devices)])  4.45 us
    ppermute x3, waiting for transfers between devices, swaps(): lax.ppermute(parts[r], axis, [(i, i ^ r) for i in range(devices)])  4.09 us
    pallas_call x1, Pallas kernels, body(): pl.pallas_call(prepare_kernel, out_shape=(matrix, matrix, shape(rows, acr...  1.65 us
    ppermute x5, waiting for transfers between devices, meet(): return lax.ppermute(x, 'trench', pairs + [(j, i) for i, j in pairs])  1.25 us
    pallas_call x1, Pallas kernels, body(): pl.pallas_call(functools.partial(sensors_kernel, rows), out_shape=slot_sh...  1.07 us
    pallas_call x1, Pallas kernels, body(): pl.pallas_call(prior_kernel, out_shape=shape(STEPS * blocks, rows // bloc...  0.74 us
    pallas_call x1, Pallas kernels, body(): pl.pallas_call(functools.partial(advance_kernel, tiles), out_shape=(shape...  0.62 us
  transfers between devices with their start and end apart: 8, of which 4 were waited for; matrix products, arithmetic and copies ran while one was open for 0% of the time, Pallas kernels for 16%

profile of v2, /device:TPU:0, one launch (start us, length us, event | category | flops | bytes accessed | tf_op | source)
XLA Modules:
  0.0 19.9 jit_solution(14971387637318719059)
XLA Ops:
  0.0 0.5 %collective-permute-start = (f32[8,4,32]{2,1,0:T(4,128)}, f32[8,4,32]{2,1,0:T(4,128)S(1)}, u32[]{:S(2)}, u32[]{:S(2)}) collective-permute-start(f32[8,4,32]{2,1,0:T(4,128)} %bitcast.4), channel_id=1, source_target_pairs={{4,0},{12,8},{20,16},{28,24},{0,4},{8,12},{16,20},{24,28},{5,1},{1... | collective-permute-start | bytes 12296 | tf_op jit(solution)/shard_map/ppermute | solution.py:363
  0.5 1.7 %prepare.1 = (bf16[192,240]{1,0:T(8,128)(2,1)S(1)}, bf16[192,240]{1,0:T(8,128)(2,1)S(1)}, f32[16,512]{1,0:T(8,128)S(1)}, f32[32,512]{1,0:T(8,128)S(1)}, f32[8,51...) custom-call(s32[16,512]{1,0:T(8,128)} %depth.1, ...), custom_call_target="tpu_custom_call" | custom-call | flops 10000000 | bytes 4000000 | tf_op jit(solution)/shard_map/prepare/pallas_call | solution.py:367
  2.1 0.0 collective-permute-done.partner
  2.1 0.0 copy-start
  2.1 0.6 %contract.1 = (f32[11,16,512]{2,1,0:T(8,128)S(1)}, f32[17,512]{1,0:T(8,128)S(1)}, f32[21,512]{1,0:T(8,128)S(1)}, f32[4,192]{1,0:T(4,128)S(1)}, f32[4,192]{1,0:T(4,128)S(1)}) custom-call(f32[1,30,16,512]{3,2,1,0:T(8,128)S(1)} %get-tuple-element.26.eta, f32[1,30,16,512]{3,2,1,0:T(8,128)S(1)} %get-tuple-element.27.flow, ...), custom_call_target="tpu_custom_call" | custom-call | flops 1000000000 | bytes 4000000 | tf_op jit(solution)/shard_map/contract/pallas_call | solution.py:401
  2.7 0.0 copy-start.1
  2.7 3.6 %collective-permute-start.2 = (f32[21,512]{1,0:T(8,128)S(1)}, f32[21,512]{1,0:T(8,128)S(1)}, u32[]{:S(2)}, u32[]{:S(2)}) collective-permute-start(f32[21,512]{1,0:T(8,128)S(1)} %get-tuple-element.37), channel_id=1, source_target_pairs={{4,8},{12,16},{20,24},{28,0},{8,4},{16,12},{24,20},{0,28},{5,9},{1... | collective-permute-start | bytes 129032 | tf_op jit(solution)/shard_map/ppermute | solution.py:363
  6.3 0.0 collective-permute-start.1
  6.3 0.6 %collective-permute-start.4 = (f32[4,192]{1,0:T(4,128)S(1)}, f32[4,192]{1,0:T(4,128)S(1)}, u32[]{:S(2)}, u32[]{:S(2)}) collective-permute-start(f32[4,192]{1,0:T(4,128)S(1)} %get-tuple-element.41), channel_id=1, source_target_pairs={{4,16},{12,24},{20,0},{28,8},{16,4},{24,12},{0,20},{8,28},{5,17},{... | collective-permute-start | bytes 9224 | tf_op jit(solution)/shard_map/ppermute | solution.py:363
  6.9 0.2 %collective-permute-start.3 = (f32[4,192]{1,0:T(4,128)S(1)}, f32[4,192]{1,0:T(4,128)S(1)}, u32[]{:S(2)}, u32[]{:S(2)}) collective-permute-start(f32[4,192]{1,0:T(4,128)S(1)} %get-tuple-element.38), channel_id=1, source_target_pairs={{4,24},{12,0},{20,8},{28,16},{24,4},{0,12},{8,20},{16,28},{5,25},{... | collective-permute-start | bytes 9224 | tf_op jit(solution)/shard_map/ppermute | solution.py:363
  7.2 1.1 %sensors.1 = (bf16[512,576]{1,0:T(8,128)(2,1)S(1)}, s32[8,576]{1,0:T(8,128)S(1)}, bf16[512,192]{1,0:T(8,128)(2,1)S(1)}, s32[8,192]{1,0:T(8,128)S(1)}) custom-call(s32[8,8,32]{2,1,0:T(8,128)S(1)} %copy-done, s32[8,8]{1,0:T(8,128)S(1)} %copy-done.1), custom_call_target="tpu_custom_call" | custom-call | flops 1000000 | bytes 2000000 | tf_op jit(solution)/shard_map/sensors/pallas_call | solution.py:421
  8.2 1.1 %collective-permute-done.4.refs_1_ = f32[4,192]{1,0:T(4,128)S(1)} collective-permute-done((f32[4,192]{1,0:T(4,128)S(1)}, f32[4,192]{1,0:T(4,128)S(1)}, u32[]{:S(2)}, u32[]{:S(2)}) %collective-permute-start.4) | collective-permute-done | bytes 3104 | tf_op jit(solution)/shard_map/ppermute | solution.py:363
  9.4 0.0 collective-permute-done.2.refs_0_.facing_out
  9.4 0.5 %inject.1.planes = f32[128,512]{1,0:T(8,128)S(1)} custom-call(bf16[512,576]{1,0:T(8,128)(2,1)S(1)} %get-tuple-element.39.hot, s32[8,576]{1,0:T(8,128)S(1)} %get-tuple-element.40.places, f32[8,4,32]{2,1,0:T(4,128)S(1)} %get-tuple-element.31.own, f32[8,4,32]{2,1,0:T(4,128)S(1)} %collective-permute-done.partner, ...), custom_call_target="tpu_custom_call" | custom-call | flops 1000 | bytes 1000 | tf_op jit(solution)/shard_map/inject/pallas_call | solution.py:430
  9.9 0.1 collective-permute-done.3.last
  10.0 0.0 collective-permute-done.1.facing_in
  10.0 0.6 %advance.1 = (f32[16,512]{1,0:T(8,128)S(1)}, f32[16,512]{1,0:T(8,128)S(1)}, f32[16,512]{1,0:T(8,128)S(1)}, f32[16,512]{1,0:T(8,128)S(1)}) custom-call(f32[11,16,512]{2,1,0:T(8,128)S(1)} %get-tuple-element.32.fields, f32[16,512]{1,0:T(8,128)S(1)} %get-tuple-element.30.cel, f32[32,512]{1,0:T(8,128)S(1)} %get-tuple-element.33.coef, ...), custom_call_target="tpu_custom_call" | custom-call | tf_op jit(solution)/shard_map/advance/pallas_call | solution.py:439
  10.6 3.7 %collective-permute-start.5 = (f32[16,512]{1,0:T(8,128)S(1)}, f32[16,512]{1,0:T(8,128)S(1)}, u32[]{:S(2)}, u32[]{:S(2)}) collective-permute-start(f32[16,512]{1,0:T(8,128)S(1)} %get-tuple-element.42), channel_id=1, source_target_pairs={{0,3},{1,2},{2,1},{3,0},{4,7},{5,6},{6,5},{7,4},{8,11},{9,10},{10,... | collective-permute-start | bytes 98312 | tf_op jit(solution)/shard_map/ppermute | solution.py:354
  14.3 0.0 collective-permute-start.6
  14.3 0.8 %collective-permute-start.7 = (f32[16,512]{1,0:T(8,128)S(1)}, f32[16,512]{1,0:T(8,128)S(1)}, u32[]{:S(2)}, u32[]{:S(2)}) collective-permute-start(f32[16,512]{1,0:T(8,128)S(1)} %get-tuple-element.44), channel_id=1, source_target_pairs={{0,1},{1,0},{2,3},{3,2},{4,5},{5,4},{6,7},{7,6},{8,9},{9,8},{10,11... | collective-permute-start | bytes 98312 | tf_op jit(solution)/shard_map/ppermute | solution.py:354
  15.1 1.6 %collective-permute-done.5.refs_0_ = f32[16,512]{1,0:T(8,128)S(1)} collective-permute-done((f32[16,512]{1,0:T(8,128)S(1)}, f32[16,512]{1,0:T(8,128)S(1)}, u32[]{:S(2)}, u32[]{:S(2)}) %collective-permute-start.5) | collective-permute-done | bytes 32800 | tf_op jit(solution)/shard_map/ppermute | solution.py:354
  16.7 2.5 %collective-permute-done.6.refs_1_ = f32[16,512]{1,0:T(8,128)S(1)} collective-permute-done((f32[16,512]{1,0:T(8,128)S(1)}, f32[16,512]{1,0:T(8,128)S(1)}, u32[]{:S(2)}, u32[]{:S(2)}) %collective-permute-start.6) | collective-permute-done | bytes 32800 | tf_op jit(solution)/shard_map/ppermute | solution.py:354
  19.2 0.0 collective-permute-done.7.refs_2_
  19.2 0.7 %prior.1 = f32[16,4,512]{2,1,0:T(4,128)} custom-call(f32[16,512]{1,0:T(8,128)S(1)} %collective-permute-done.5.refs_0_, f32[16,512]{1,0:T(8,128)S(1)} %collective-permute-done.6.refs_1_, f32[16,512]{1,0:T(8,128)S(1)} %collective-permute-done.7.refs_2_, f32[16,512]{1,0:T(8,128)S(1)} %get-tuple-element.45.refs_3_, f32[8,512]{1,0:T(8,128)S(1)} %get-tuple-element.46.refs_4_), custom_call_target="tpu_custom_call" | custom-call | tf_op jit(solution)/shard_map/prior/pallas_call | solution.py:453
  (2 shorter events, 0.0 us)
Async XLA Ops:
  0.0 2.1 %collective-permute-start = (f32[8,4,32]{2,1,0:T(4,128)}, f32[8,4,32]{2,1,0:T(4,128)S(1)}, u32[]{:S(2)}, u32[]{:S(2)}) collective-permute-start(f32[8,4,32]{2,1,0:T(4,128)} %bitcast.4), channel_id=1, source_target_pairs={{4,0},{12,8},{20,16},{28,24},{0,4},{8,12},{16,20},{24,28},{5,1},{1... | collective-permute-start | bytes 12296 | tf_op jit(solution)/shard_map/ppermute | solution.py:363
  2.1 5.0 %copy-start = (s32[8,8,32]{2,1,0:T(8,128)S(1)}, s32[8,8,32]{2,1,0:T(8,128)}, u32[]{:S(2)}) copy-start(s32[8,8,32]{2,1,0:T(8,128)} %cells.1) | copy-start | bytes 24580
  2.7 4.5 %copy-start.1 = (s32[8,8]{1,0:T(8,128)S(1)}, s32[8,8]{1,0:T(8,128)}, u32[]{:S(2)}) copy-start(s32[8,8]{1,0:T(8,128)} %count.1) | copy-start | bytes 772
  2.7 6.7 %collective-permute-start.2 = (f32[21,512]{1,0:T(8,128)S(1)}, f32[21,512]{1,0:T(8,128)S(1)}, u32[]{:S(2)}, u32[]{:S(2)}) collective-permute-start(f32[21,512]{1,0:T(8,128)S(1)} %get-tuple-element.37), channel_id=1, source_target_pairs={{4,8},{12,16},{20,24},{28,0},{8,4},{16,12},{24,20},{0,28},{5,9},{1... | collective-permute-start | bytes 129032 | tf_op jit(solution)/shard_map/ppermute | solution.py:363
  6.3 3.7 %collective-permute-start.1 = (f32[17,512]{1,0:T(8,128)S(1)}, f32[17,512]{1,0:T(8,128)S(1)}, u32[]{:S(2)}, u32[]{:S(2)}) collective-permute-start(f32[17,512]{1,0:T(8,128)S(1)} %get-tuple-element.36), channel_id=1, source_target_pairs={{4,0},{12,8},{20,16},{28,24},{0,4},{8,12},{16,20},{24,28},{5,1},{1... | collective-permute-start | bytes 104456 | tf_op jit(solution)/shard_map/ppermute | solution.py:363
  6.3 3.0 %collective-permute-start.4 = (f32[4,192]{1,0:T(4,128)S(1)}, f32[4,192]{1,0:T(4,128)S(1)}, u32[]{:S(2)}, u32[]{:S(2)}) collective-permute-start(f32[4,192]{1,0:T(4,128)S(1)} %get-tuple-element.41), channel_id=1, source_target_pairs={{4,16},{12,24},{20,0},{28,8},{16,4},{24,12},{0,20},{8,28},{5,17},{... | collective-permute-start | bytes 9224 | tf_op jit(solution)/shard_map/ppermute | solution.py:363
  6.9 3.0 %collective-permute-start.3 = (f32[4,192]{1,0:T(4,128)S(1)}, f32[4,192]{1,0:T(4,128)S(1)}, u32[]{:S(2)}, u32[]{:S(2)}) collective-permute-start(f32[4,192]{1,0:T(4,128)S(1)} %get-tuple-element.38), channel_id=1, source_target_pairs={{4,24},{12,0},{20,8},{28,16},{24,4},{0,12},{8,20},{16,28},{5,25},{... | collective-permute-start | bytes 9224 | tf_op jit(solution)/shard_map/ppermute | solution.py:363
  10.6 6.1 %collective-permute-start.5 = (f32[16,512]{1,0:T(8,128)S(1)}, f32[16,512]{1,0:T(8,128)S(1)}, u32[]{:S(2)}, u32[]{:S(2)}) collective-permute-start(f32[16,512]{1,0:T(8,128)S(1)} %get-tuple-element.42), channel_id=1, source_target_pairs={{0,3},{1,2},{2,1},{3,0},{4,7},{5,6},{6,5},{7,4},{8,11},{9,10},{10,... | collective-permute-start | bytes 98312 | tf_op jit(solution)/shard_map/ppermute | solution.py:354
  14.3 4.9 %collective-permute-start.6 = (f32[16,512]{1,0:T(8,128)S(1)}, f32[16,512]{1,0:T(8,128)S(1)}, u32[]{:S(2)}, u32[]{:S(2)}) collective-permute-start(f32[16,512]{1,0:T(8,128)S(1)} %get-tuple-element.43), channel_id=1, source_target_pairs={{0,2},{1,3},{2,0},{3,1},{4,6},{5,7},{6,4},{7,5},{8,10},{9,11},{10,... | collective-permute-start | bytes 98312 | tf_op jit(solution)/shard_map/ppermute | solution.py:354
  14.3 4.9 %collective-permute-start.7 = (f32[16,512]{1,0:T(8,128)S(1)}, f32[16,512]{1,0:T(8,128)S(1)}, u32[]{:S(2)}, u32[]{:S(2)}) collective-permute-start(f32[16,512]{1,0:T(8,128)S(1)} %get-tuple-element.44), channel_id=1, source_target_pairs={{0,1},{1,0},{2,3},{3,2},{4,5},{5,4},{6,7},{7,6},{8,9},{9,8},{10,11... | collective-permute-start | bytes 98312 | tf_op jit(solution)/shard_map/ppermute | solution.py:354

commit v3 on v2

--- a/solution.py
+++ b/solution.py
@@ -35,9 +35,9 @@
 
 
 def prepare_kernel(
-    depth, table, damping, profile, band, residual, eta, flow,
-    w_eta, w_flow, cel, coef, factor, own, eta_v, flow_v,
-    depth_v, table_s, damping_v, profile_v, band_v, sems,
+    depth, table, damping, profile, band, cells, count, residual, eta, flow,
+    w_eta, w_flow, cel, coef, factor, hot_early, places_early, hot_late, places_late, own, eta_v, flow_v,
+    depth_v, table_s, damping_v, profile_v, band_v, cells_v, count_s, sems,
 ):
     rows, across = cel.shape
     levels = damping.shape[1]
@@ -45,7 +45,7 @@
         pltpu.make_async_copy(src, dst, sems.at[i])
         for i, (src, dst) in enumerate((
             (damping, damping_v), (profile, profile_v), (table, table_s), (depth, depth_v),
-            (band, band_v), (residual, own), (eta, eta_v), (flow, flow_v),
+            (band, band_v), (cells, cells_v), (count, count_s), (residual, own), (eta, eta_v), (flow, flow_v),
         ))
     ]
     for copy in copies:
@@ -103,6 +103,7 @@
     w_eta[...] = matrix(us)
     w_flow[...] = matrix(vs)
 
+    list_sensors(rows, cells_v, count_s, hot_early, places_early, hot_late, places_late)
     for copy in copies[-2:]:
         copy.wait()
 
@@ -152,8 +153,11 @@
 
 
 def sources(me, tiles):
-    listed = [met(me, d, tiles) ^ core for d in range(tiles // 2) for core in range(2)]
-    return listed[:-2], listed[-2:]
+    def at(distances):
+        return [met(me, d, tiles) ^ core for d in distances for core in range(2)]
+
+    half = tiles // 4
+    return at(d for d in range(tiles // 2) if d != half), at([half])
 
 
 def widen(values, lanes):
@@ -172,7 +176,7 @@
     return jnp.concatenate([residual_rows(owner, own), residual_rows(owner, partner)], axis=1)
 
 
-def sensors_kernel(rows, cells, count, hot_early, places_early, hot_late, places_late):
+def list_sensors(rows, cells, count, hot_early, places_early, hot_late, places_late):
     me = lax.axis_index("trench")
     tiles, _, slots = cells.shape
     across = hot_early.shape[0]
@@ -363,8 +367,11 @@
         return lax.ppermute(x, "trench", pairs + [(j, i) for i, j in pairs])
 
     partner = meet(own, 0)
+    def slot_shapes(count):
+        return shape(across, 3 * slots * count, dtype=jnp.bfloat16), shape(8, 3 * slots * count, dtype=jnp.int32)
+
     matrix = shape(16 * (len(FIELDS) + 1), 8 * levels, dtype=jnp.bfloat16)
-    w_eta, w_flow, cel, coef, factor, own, eta, flow = pl.pallas_call(
+    w_eta, w_flow, cel, coef, factor, hot, places, hot_late, places_late, own, eta, flow = pl.pallas_call(
         prepare_kernel,
         out_shape=(
             matrix,
@@ -372,19 +379,23 @@
             shape(rows, across),
             shape(8 * STEPS, across),
             shape(band_weight.shape[0], across),
+            *slot_shapes(tiles - 2),
+            *slot_shapes(2),
             shape(*own.shape),
             shape(*adjoint_eta.shape),
             shape(*adjoint_flow.shape),
         ),
-        in_specs=[spec(pltpu.HBM)] * 8,
-        out_specs=(spec(VMEM),) * 8,
+        in_specs=[spec(pltpu.HBM)] * 10,
+        out_specs=(spec(VMEM),) * 12,
         scratch_shapes=[
             VMEM((rows, across), jnp.int32),
             SMEM(speed_table.shape, jnp.float32),
             VMEM((1, levels), jnp.float32),
             VMEM((1, levels), jnp.float32),
             VMEM((1, band_weight.shape[0]), jnp.float32),
-            pltpu.SemaphoreType.DMA((8,)),
+            VMEM(sensor_cell.shape, jnp.int32),
+            SMEM(sensor_count.shape, jnp.int32),
+            pltpu.SemaphoreType.DMA((10,)),
         ],
         compiler_params=params,
         cost_estimate=pl.CostEstimate(flops=10**7, bytes_accessed=4 * 10**6, transcendentals=0),
@@ -394,7 +405,7 @@
             pltpu.with_memory_space_constraint(x, pltpu.HBM)
             for x in (
                 depth_class, speed_table, damping[None], profile[None], band_weight[None],
-                own, adjoint_eta, adjoint_flow,
+                sensor_cell, sensor_count, own, adjoint_eta, adjoint_flow,
             )
         ]
     )
@@ -412,30 +423,20 @@
         name="contract",
     )(eta, flow, w_eta, w_flow, cel, own, partner)
     facing_out = meet(outer, 1)
-    gots = [facing_out] + [meet(relay, d) for d, relay in enumerate(relays, 2)]
+    gots = {d: meet(relay, d) for d, relay in enumerate(relays, 2)}
+    last = gots.pop(chips // 2)
+    gots = [facing_out, *gots.values()]
     facing_in = meet(inner, 0)
 
-    def slot_shapes(count):
-        return shape(across, 3 * slots * count, dtype=jnp.bfloat16), shape(8, 3 * slots * count, dtype=jnp.int32)
-
-    hot, places, hot_late, places_late = pl.pallas_call(
-        functools.partial(sensors_kernel, rows),
-        out_shape=slot_shapes(tiles - 2) + slot_shapes(2),
-        in_specs=[spec(VMEM), spec(SMEM)],
-        out_specs=(spec(VMEM),) * 4,
-        compiler_params=params,
-        cost_estimate=pl.CostEstimate(flops=10**6, bytes_accessed=2 * 10**6, transcendentals=0),
-        name="sensors",
-    )(sensor_cell, sensor_count)
     planes = pl.pallas_call(
         inject_kernel,
         out_shape=shape(STEPS * (rows + 2 * PAD), across),
-        in_specs=[spec(VMEM)] * (3 + len(gots)),
+        in_specs=[spec(VMEM)] * (4 + len(gots)),
         out_specs=spec(VMEM),
         compiler_params=params,
         cost_estimate=pl.CostEstimate(flops=1000, bytes_accessed=1000, transcendentals=0),
         name="inject",
-    )(hot, places, own, partner, *gots[:-1])
+    )(hot, places, own, partner, *gots)
     series = pl.pallas_call(
         functools.partial(advance_kernel, tiles),
         out_shape=(shape(STEPS * rows // blocks, across),) * blocks,
@@ -448,7 +449,7 @@
         ],
         compiler_params=params,
         name="advance",
-    )(fields, cel, coef, hot_late, places_late, facing_in, facing_out, gots[-1], planes)
+    )(fields, cel, coef, hot_late, places_late, facing_in, facing_out, last, planes)
     gots = swaps(series, "tblock")
     return pl.pallas_call(
         prior_kernel,

time: 20.1 us -> 20.2 us (level)
  starting transfers between devices: 9.35 us -> 10.3 us
  Pallas kernels: 5.13 us -> 4.18 us
    pallas_call x1 -> x0, Pallas kernels: 1.07 us -> none  [body(): pl.pallas_call(functools.partial(sensors_kernel, rows), out_shape=slot_sh...]
    ppermute x5, starting transfers between devices: 4.9 us -> 5.81 us  [meet(): return lax.ppermute(x, 'trench', pairs + [(j, i) for i, j in pairs])]
  transfers between devices with their start and end apart: 8 -> 8, of which waited for: 4 -> 3; matrix products, arithmetic and copies ran while one was open for 0% -> 0% of each run, Pallas kernels for 16% -> 11%
where the time goes in v3:
time: 20.2 us; the launch traced here: 20 us
  starting transfers between devices  10.3 us (51%)
  waiting for transfers between devices  5.53 us (27%)
  Pallas kernels  4.18 us (21%)
    ppermute x5, starting transfers between devices, meet(): return lax.ppermute(x, 'trench', pairs + [(j, i) for i, j in pairs])  5.81 us
    ppermute x3, starting transfers between devices, swaps(): lax.ppermute(parts[r], axis, [(i, i ^ r) for i in range(devices)])  4.45 us
    ppermute x3, waiting for transfers between devices, swaps(): lax.ppermute(parts[r], axis, [(i, i ^ r) for i in range(devices)])  4.21 us
    pallas_call x1, Pallas kernels, body(): pl.pallas_call(prepare_kernel, out_shape=(matrix, matrix, shape(rows, acr...  1.78 us
    ppermute x5, waiting for transfers between devices, meet(): return lax.ppermute(x, 'trench', pairs + [(j, i) for i, j in pairs])  1.33 us
    pallas_call x1, Pallas kernels, body(): pl.pallas_call(prior_kernel, out_shape=shape(STEPS * blocks, rows // bloc...  0.74 us
    pallas_call x1, Pallas kernels, body(): pl.pallas_call(functools.partial(advance_kernel, tiles), out_shape=(shape...  0.63 us
    pallas_call x1, Pallas kernels, body(): pl.pallas_call(contract_kernel, out_shape=(shape(len(FIELDS), rows, acros...  0.55 us
  transfers between devices with their start and end apart: 8, of which 3 were waited for; matrix products, arithmetic and copies ran while one was open for 0% of the time, Pallas kernels for 11%

profile of v3, /device:TPU:0, one launch (start us, length us, event | category | flops | bytes accessed | tf_op | source)
XLA Modules:
  0.0 20.0 jit_solution(1423062883776550958)
XLA Ops:
  0.0 0.5 %collective-permute-start = (f32[8,4,32]{2,1,0:T(4,128)}, f32[8,4,32]{2,1,0:T(4,128)S(1)}, u32[]{:S(2)}, u32[]{:S(2)}) collective-permute-start(f32[8,4,32]{2,1,0:T(4,128)} %bitcast.4), channel_id=1, source_target_pairs={{4,0},{12,8},{20,16},{28,24},{0,4},{8,12},{16,20},{24,28},{5,1},{1... | collective-permute-start | bytes 12296 | tf_op jit(solution)/shard_map/ppermute | solution.py:367
  0.5 1.8 %prepare.1 = (bf16[192,240]{1,0:T(8,128)(2,1)S(1)}, bf16[192,240]{1,0:T(8,128)(2,1)S(1)}, f32[16,512]{1,0:T(8,128)S(1)}, f32[32,512]{1,0:T(8,128)S(1)}, f32[8,51...) custom-call(s32[16,512]{1,0:T(8,128)} %depth.1, ...), custom_call_target="tpu_custom_call" | custom-call | flops 10000000 | bytes 4000000 | tf_op jit(solution)/shard_map/prepare/pallas_call | solution.py:374
  2.2 0.0 collective-permute-done.partner
  2.2 0.5 %contract.1 = (f32[11,16,512]{2,1,0:T(8,128)S(1)}, f32[17,512]{1,0:T(8,128)S(1)}, f32[21,512]{1,0:T(8,128)S(1)}, f32[4,192]{1,0:T(4,128)S(1)}, f32[4,192]{1,0:T(4,128)S(1)}) custom-call(f32[1,30,16,512]{3,2,1,0:T(8,128)S(1)} %get-tuple-element.26.eta, f32[1,30,16,512]{3,2,1,0:T(8,128)S(1)} %get-tuple-element.27.flow, ...), custom_call_target="tpu_custom_call" | custom-call | flops 1000000000 | bytes 4000000 | tf_op jit(solution)/shard_map/contract/pallas_call | solution.py:412
  2.8 3.6 %collective-permute-start.2 = (f32[21,512]{1,0:T(8,128)S(1)}, f32[21,512]{1,0:T(8,128)S(1)}, u32[]{:S(2)}, u32[]{:S(2)}) collective-permute-start(f32[21,512]{1,0:T(8,128)S(1)} %get-tuple-element.37), channel_id=1, source_target_pairs={{4,8},{12,16},{20,24},{28,0},{8,4},{16,12},{24,20},{0,28},{5,9},{1... | collective-permute-start | bytes 129032 | tf_op jit(solution)/shard_map/ppermute | solution.py:367
  6.4 0.0 collective-permute-start.1
  6.4 0.1 collective-permute-start.4
  6.6 1.6 %collective-permute-start.3 = (f32[4,192]{1,0:T(4,128)S(1)}, f32[4,192]{1,0:T(4,128)S(1)}, u32[]{:S(2)}, u32[]{:S(2)}) collective-permute-start(f32[4,192]{1,0:T(4,128)S(1)} %get-tuple-element.38), channel_id=1, source_target_pairs={{4,16},{12,24},{20,0},{28,8},{16,4},{24,12},{0,20},{8,28},{5,17},{... | collective-permute-start | bytes 9224 | tf_op jit(solution)/shard_map/ppermute | solution.py:367
  8.2 1.3 %collective-permute-done.4.refs_1_ = f32[4,192]{1,0:T(4,128)S(1)} collective-permute-done((f32[4,192]{1,0:T(4,128)S(1)}, f32[4,192]{1,0:T(4,128)S(1)}, u32[]{:S(2)}, u32[]{:S(2)}) %collective-permute-start.4) | collective-permute-done | bytes 3104 | tf_op jit(solution)/shard_map/ppermute | solution.py:367
  9.5 0.0 collective-permute-done.2.refs_0_.facing_out
  9.5 0.5 %inject.1.planes = f32[128,512]{1,0:T(8,128)S(1)} custom-call(bf16[512,576]{1,0:T(8,128)(2,1)S(1)} %get-tuple-element.39.hot, s32[8,576]{1,0:T(8,128)S(1)} %get-tuple-element.40.places, f32[8,4,32]{2,1,0:T(4,128)S(1)} %get-tuple-element.31.own, f32[8,4,32]{2,1,0:T(4,128)S(1)} %collective-permute-done.partner, ...), custom_call_target="tpu_custom_call" | custom-call | flops 1000 | bytes 1000 | tf_op jit(solution)/shard_map/inject/pallas_call | solution.py:431
  10.0 0.0 collective-permute-done.3.last
  10.0 0.0 collective-permute-done.1.facing_in
  10.0 0.6 %advance.1 = (f32[16,512]{1,0:T(8,128)S(1)}, f32[16,512]{1,0:T(8,128)S(1)}, f32[16,512]{1,0:T(8,128)S(1)}, f32[16,512]{1,0:T(8,128)S(1)}) custom-call(f32[11,16,512]{2,1,0:T(8,128)S(1)} %get-tuple-element.32.fields, f32[16,512]{1,0:T(8,128)S(1)} %get-tuple-element.30.cel, f32[32,512]{1,0:T(8,128)S(1)} %get-tuple-element.33.coef, ...), custom_call_target="tpu_custom_call" | custom-call | tf_op jit(solution)/shard_map/advance/pallas_call | solution.py:440
  10.6 3.7 %collective-permute-start.5 = (f32[16,512]{1,0:T(8,128)S(1)}, f32[16,512]{1,0:T(8,128)S(1)}, u32[]{:S(2)}, u32[]{:S(2)}) collective-permute-start(f32[16,512]{1,0:T(8,128)S(1)} %get-tuple-element.42), channel_id=1, source_target_pairs={{0,3},{1,2},{2,1},{3,0},{4,7},{5,6},{6,5},{7,4},{8,11},{9,10},{10,... | collective-permute-start | bytes 98312 | tf_op jit(solution)/shard_map/ppermute | solution.py:358
  14.3 0.0 collective-permute-start.6
  14.3 0.8 %collective-permute-start.7 = (f32[16,512]{1,0:T(8,128)S(1)}, f32[16,512]{1,0:T(8,128)S(1)}, u32[]{:S(2)}, u32[]{:S(2)}) collective-permute-start(f32[16,512]{1,0:T(8,128)S(1)} %get-tuple-element.44), channel_id=1, source_target_pairs={{0,1},{1,0},{2,3},{3,2},{4,5},{5,4},{6,7},{7,6},{8,9},{9,8},{10,11... | collective-permute-start | bytes 98312 | tf_op jit(solution)/shard_map/ppermute | solution.py:358
  15.1 1.3 %collective-permute-done.5.refs_0_ = f32[16,512]{1,0:T(8,128)S(1)} collective-permute-done((f32[16,512]{1,0:T(8,128)S(1)}, f32[16,512]{1,0:T(8,128)S(1)}, u32[]{:S(2)}, u32[]{:S(2)}) %collective-permute-start.5) | collective-permute-done | bytes 32800 | tf_op jit(solution)/shard_map/ppermute | solution.py:358
  16.4 2.9 %collective-permute-done.6.refs_1_ = f32[16,512]{1,0:T(8,128)S(1)} collective-permute-done((f32[16,512]{1,0:T(8,128)S(1)}, f32[16,512]{1,0:T(8,128)S(1)}, u32[]{:S(2)}, u32[]{:S(2)}) %collective-permute-start.6) | collective-permute-done | bytes 32800 | tf_op jit(solution)/shard_map/ppermute | solution.py:358
  19.3 0.0 collective-permute-done.7.refs_2_
  19.3 0.7 %prior.1 = f32[16,4,512]{2,1,0:T(4,128)} custom-call(f32[16,512]{1,0:T(8,128)S(1)} %collective-permute-done.5.refs_0_, f32[16,512]{1,0:T(8,128)S(1)} %collective-permute-done.6.refs_1_, f32[16,512]{1,0:T(8,128)S(1)} %collective-permute-done.7.refs_2_, f32[16,512]{1,0:T(8,128)S(1)} %get-tuple-element.45.refs_3_, f32[8,512]{1,0:T(8,128)S(1)} %get-tuple-element.46.refs_4_), custom_call_target="tpu_custom_call" | custom-call | tf_op jit(solution)/shard_map/prior/pallas_call | solution.py:454
Async XLA Ops:
  0.0 2.2 %collective-permute-start = (f32[8,4,32]{2,1,0:T(4,128)}, f32[8,4,32]{2,1,0:T(4,128)S(1)}, u32[]{:S(2)}, u32[]{:S(2)}) collective-permute-start(f32[8,4,32]{2,1,0:T(4,128)} %bitcast.4), channel_id=1, source_target_pairs={{4,0},{12,8},{20,16},{28,24},{0,4},{8,12},{16,20},{24,28},{5,1},{1... | collective-permute-start | bytes 12296 | tf_op jit(solution)/shard_map/ppermute | solution.py:367
  2.8 6.7 %collective-permute-start.2 = (f32[21,512]{1,0:T(8,128)S(1)}, f32[21,512]{1,0:T(8,128)S(1)}, u32[]{:S(2)}, u32[]{:S(2)}) collective-permute-start(f32[21,512]{1,0:T(8,128)S(1)} %get-tuple-element.37), channel_id=1, source_target_pairs={{4,8},{12,16},{20,24},{28,0},{8,4},{16,12},{24,20},{0,28},{5,9},{1... | collective-permute-start | bytes 129032 | tf_op jit(solution)/shard_map/ppermute | solution.py:367
  6.4 3.5 %collective-permute-start.1 = (f32[17,512]{1,0:T(8,128)S(1)}, f32[17,512]{1,0:T(8,128)S(1)}, u32[]{:S(2)}, u32[]{:S(2)}) collective-permute-start(f32[17,512]{1,0:T(8,128)S(1)} %get-tuple-element.36), channel_id=1, source_target_pairs={{4,0},{12,8},{20,16},{28,24},{0,4},{8,12},{16,20},{24,28},{5,1},{1... | collective-permute-start | bytes 104456 | tf_op jit(solution)/shard_map/ppermute | solution.py:367
  6.4 3.0 %collective-permute-start.4 = (f32[4,192]{1,0:T(4,128)S(1)}, f32[4,192]{1,0:T(4,128)S(1)}, u32[]{:S(2)}, u32[]{:S(2)}) collective-permute-start(f32[4,192]{1,0:T(4,128)S(1)} %get-tuple-element.41), channel_id=1, source_target_pairs={{4,24},{12,0},{20,8},{28,16},{24,4},{0,12},{8,20},{16,28},{5,25},{... | collective-permute-start | bytes 9224 | tf_op jit(solution)/shard_map/ppermute | solution.py:367
  6.6 3.4 %collective-permute-start.3 = (f32[4,192]{1,0:T(4,128)S(1)}, f32[4,192]{1,0:T(4,128)S(1)}, u32[]{:S(2)}, u32[]{:S(2)}) collective-permute-start(f32[4,192]{1,0:T(4,128)S(1)} %get-tuple-element.38), channel_id=1, source_target_pairs={{4,16},{12,24},{20,0},{28,8},{16,4},{24,12},{0,20},{8,28},{5,17},{... | collective-permute-start | bytes 9224 | tf_op jit(solution)/shard_map/ppermute | solution.py:367
  10.6 5.8 %collective-permute-start.5 = (f32[16,512]{1,0:T(8,128)S(1)}, f32[16,512]{1,0:T(8,128)S(1)}, u32[]{:S(2)}, u32[]{:S(2)}) collective-permute-start(f32[16,512]{1,0:T(8,128)S(1)} %get-tuple-element.42), channel_id=1, source_target_pairs={{0,3},{1,2},{2,1},{3,0},{4,7},{5,6},{6,5},{7,4},{8,11},{9,10},{10,... | collective-permute-start | bytes 98312 | tf_op jit(solution)/shard_map/ppermute | solution.py:358
  14.3 5.0 %collective-permute-start.6 = (f32[16,512]{1,0:T(8,128)S(1)}, f32[16,512]{1,0:T(8,128)S(1)}, u32[]{:S(2)}, u32[]{:S(2)}) collective-permute-start(f32[16,512]{1,0:T(8,128)S(1)} %get-tuple-element.43), channel_id=1, source_target_pairs={{0,2},{1,3},{2,0},{3,1},{4,6},{5,7},{6,4},{7,5},{8,10},{9,11},{10,... | collective-permute-start | bytes 98312 | tf_op jit(solution)/shard_map/ppermute | solution.py:358
  14.3 5.0 %collective-permute-start.7 = (f32[16,512]{1,0:T(8,128)S(1)}, f32[16,512]{1,0:T(8,128)S(1)}, u32[]{:S(2)}, u32[]{:S(2)}) collective-permute-start(f32[16,512]{1,0:T(8,128)S(1)} %get-tuple-element.44), channel_id=1, source_target_pairs={{0,1},{1,0},{2,3},{3,2},{4,5},{5,4},{6,7},{7,6},{8,9},{9,8},{10,11... | collective-permute-start | bytes 98312 | tf_op jit(solution)/shard_map/ppermute | solution.py:358

commit v4 on v3

--- a/solution.py
+++ b/solution.py
@@ -157,7 +157,7 @@
         return [met(me, d, tiles) ^ core for d in distances for core in range(2)]
 
     half = tiles // 4
-    return at(d for d in range(tiles // 2) if d != half), at([half])
+    return at(d for d in range(tiles // 2) if d not in (half, 1)), at((half, 1))
 
 
 def widen(values, lanes):
@@ -232,7 +232,9 @@
     before = jnp.where(odd, inner, outer)
     after = jnp.where(odd, outer, inner)
 
-    all_planes = planes[...] + planes_of(last[0:STEPS, 0 : hot.shape[1]], hot, places, tall)
+    per = hot.shape[1] // 2
+    values = jnp.concatenate([last[:, 0:per], facing_out[0:STEPS, 0:per]], axis=1)
+    all_planes = planes[...] + planes_of(values, hot, places, tall)
     inject = [all_planes[tall * t : tall * t + tall] for t in range(STEPS)]
 
     def extend(store, own, at, width):
@@ -379,8 +381,8 @@
             shape(rows, across),
             shape(8 * STEPS, across),
             shape(band_weight.shape[0], across),
-            *slot_shapes(tiles - 2),
-            *slot_shapes(2),
+            *slot_shapes(tiles - 4),
+            *slot_shapes(4),
             shape(*own.shape),
             shape(*adjoint_eta.shape),
             shape(*adjoint_flow.shape),
@@ -425,7 +427,7 @@
     facing_out = meet(outer, 1)
     gots = {d: meet(relay, d) for d, relay in enumerate(relays, 2)}
     last = gots.pop(chips // 2)
-    gots = [facing_out, *gots.values()]
+    gots = list(gots.values())
     facing_in = meet(inner, 0)
 
     planes = pl.pallas_call(

time: 20.2 us -> 20.1 us (level)
  no operation moved by 1% of the time
where the time goes in v4:
time: 20.1 us; the launch traced here: 20 us
  starting transfers between devices  10.2 us (51%)
  waiting for transfers between devices  5.55 us (28%)
  Pallas kernels  4.14 us (21%)
    ppermute x5, starting transfers between devices, meet(): return lax.ppermute(x, 'trench', pairs + [(j, i) for i, j in pairs])  5.79 us
    ppermute x3, starting transfers between devices, swaps(): lax.ppermute(parts[r], axis, [(i, i ^ r) for i in range(devices)])  4.45 us
    ppermute x3, waiting for transfers between devices, swaps(): lax.ppermute(parts[r], axis, [(i, i ^ r) for i in range(devices)])  4.23 us
    pallas_call x1, Pallas kernels, body(): pl.pallas_call(prepare_kernel, out_shape=(matrix, matrix, shape(rows, acr...  1.71 us
    ppermute x5, waiting for transfers between devices, meet(): return lax.ppermute(x, 'trench', pairs + [(j, i) for i, j in pairs])  1.32 us
    pallas_call x1, Pallas kernels, body(): pl.pallas_call(prior_kernel, out_shape=shape(STEPS * blocks, rows // bloc...  0.74 us
    pallas_call x1, Pallas kernels, body(): pl.pallas_call(functools.partial(advance_kernel, tiles), out_shape=(shape...  0.72 us
    pallas_call x1, Pallas kernels, body(): pl.pallas_call(contract_kernel, out_shape=(shape(len(FIELDS), rows, acros...  0.56 us
  transfers between devices with their start and end apart: 8, of which 3 were waited for; matrix products, arithmetic and copies ran while one was open for 0% of the time, Pallas kernels for 11%

profile of v4, /device:TPU:0, one launch (start us, length us, event | category | flops | bytes accessed | tf_op | source)
XLA Modules:
  0.0 20.0 jit_solution(5203641771720209167)
XLA Ops:
  0.0 0.5 %collective-permute-start = (f32[8,4,32]{2,1,0:T(4,128)}, f32[8,4,32]{2,1,0:T(4,128)S(1)}, u32[]{:S(2)}, u32[]{:S(2)}) collective-permute-start(f32[8,4,32]{2,1,0:T(4,128)} %bitcast.4), channel_id=1, source_target_pairs={{4,0},{12,8},{20,16},{28,24},{0,4},{8,12},{16,20},{24,28},{5,1},{1... | collective-permute-start | bytes 12296 | tf_op jit(solution)/shard_map/ppermute | solution.py:369
  0.5 1.7 %prepare.1 = (bf16[192,240]{1,0:T(8,128)(2,1)S(1)}, bf16[192,240]{1,0:T(8,128)(2,1)S(1)}, f32[16,512]{1,0:T(8,128)S(1)}, f32[32,512]{1,0:T(8,128)S(1)}, f32[8,51...) custom-call(s32[16,512]{1,0:T(8,128)} %depth.1, ...), custom_call_target="tpu_custom_call" | custom-call | flops 10000000 | bytes 4000000 | tf_op jit(solution)/shard_map/prepare/pallas_call | solution.py:376
  2.2 0.0 collective-permute-done.partner
  2.2 0.6 %contract.1 = (f32[11,16,512]{2,1,0:T(8,128)S(1)}, f32[17,512]{1,0:T(8,128)S(1)}, f32[21,512]{1,0:T(8,128)S(1)}, f32[4,192]{1,0:T(4,128)S(1)}, f32[4,192]{1,0:T(4,128)S(1)}) custom-call(f32[1,30,16,512]{3,2,1,0:T(8,128)S(1)} %get-tuple-element.26.eta, f32[1,30,16,512]{3,2,1,0:T(8,128)S(1)} %get-tuple-element.27.flow, ...), custom_call_target="tpu_custom_call" | custom-call | flops 1000000000 | bytes 4000000 | tf_op jit(solution)/shard_map/contract/pallas_call | solution.py:414
  2.7 3.6 %collective-permute-start.2 = (f32[21,512]{1,0:T(8,128)S(1)}, f32[21,512]{1,0:T(8,128)S(1)}, u32[]{:S(2)}, u32[]{:S(2)}) collective-permute-start(f32[21,512]{1,0:T(8,128)S(1)} %get-tuple-element.37), channel_id=1, source_target_pairs={{4,8},{12,16},{20,24},{28,0},{8,4},{16,12},{24,20},{0,28},{5,9},{1... | collective-permute-start | bytes 129032 | tf_op jit(solution)/shard_map/ppermute | solution.py:369
  6.4 0.0 collective-permute-start.1
  6.4 0.1 collective-permute-start.4
  6.5 1.6 %collective-permute-start.3 = (f32[4,192]{1,0:T(4,128)S(1)}, f32[4,192]{1,0:T(4,128)S(1)}, u32[]{:S(2)}, u32[]{:S(2)}) collective-permute-start(f32[4,192]{1,0:T(4,128)S(1)} %get-tuple-element.38), channel_id=1, source_target_pairs={{4,16},{12,24},{20,0},{28,8},{16,4},{24,12},{0,20},{8,28},{5,17},{... | collective-permute-start | bytes 9224 | tf_op jit(solution)/shard_map/ppermute | solution.py:369
  8.1 1.3 %collective-permute-done.4.refs_0_ = f32[4,192]{1,0:T(4,128)S(1)} collective-permute-done((f32[4,192]{1,0:T(4,128)S(1)}, f32[4,192]{1,0:T(4,128)S(1)}, u32[]{:S(2)}, u32[]{:S(2)}) %collective-permute-start.4) | collective-permute-done | bytes 3104 | tf_op jit(solution)/shard_map/ppermute | solution.py:369
  9.4 0.4 %inject.1.planes = f32[128,512]{1,0:T(8,128)S(1)} custom-call(bf16[512,384]{1,0:T(8,128)(2,1)S(1)} %get-tuple-element.39.hot, s32[8,384]{1,0:T(8,128)S(1)} %get-tuple-element.40.places, f32[8,4,32]{2,1,0:T(4,128)S(1)} %get-tuple-element.31.own, f32[8,4,32]{2,1,0:T(4,128)S(1)} %collective-permute-done.partner, f32[4,192]{1,0:T(4,128)S(1)} %collective-permute-done.4.refs_0_), custom_call_target="tpu_custom_call" | custom-call | flops 1000 | bytes 1000 | tf_op jit(solution)/shard_map/inject/pallas_call | solution.py:433
  9.8 0.0 collective-permute-done.3.last
  9.8 0.0 collective-permute-done.1.facing_in
  9.8 0.0 collective-permute-done.2.facing_out
  9.8 0.7 %advance.1 = (f32[16,512]{1,0:T(8,128)S(1)}, f32[16,512]{1,0:T(8,128)S(1)}, f32[16,512]{1,0:T(8,128)S(1)}, f32[16,512]{1,0:T(8,128)S(1)}) custom-call(f32[11,16,512]{2,1,0:T(8,128)S(1)} %get-tuple-element.32.fields, f32[16,512]{1,0:T(8,128)S(1)} %get-tuple-element.30.cel, f32[32,512]{1,0:T(8,128)S(1)} %get-tuple-element.33.coef, ...), custom_call_target="tpu_custom_call" | custom-call | tf_op jit(solution)/shard_map/advance/pallas_call | solution.py:442
  10.6 3.7 %collective-permute-start.5 = (f32[16,512]{1,0:T(8,128)S(1)}, f32[16,512]{1,0:T(8,128)S(1)}, u32[]{:S(2)}, u32[]{:S(2)}) collective-permute-start(f32[16,512]{1,0:T(8,128)S(1)} %get-tuple-element.42), channel_id=1, source_target_pairs={{0,3},{1,2},{2,1},{3,0},{4,7},{5,6},{6,5},{7,4},{8,11},{9,10},{10,... | collective-permute-start | bytes 98312 | tf_op jit(solution)/shard_map/ppermute | solution.py:360
  14.2 0.0 collective-permute-start.6
  14.2 0.8 %collective-permute-start.7 = (f32[16,512]{1,0:T(8,128)S(1)}, f32[16,512]{1,0:T(8,128)S(1)}, u32[]{:S(2)}, u32[]{:S(2)}) collective-permute-start(f32[16,512]{1,0:T(8,128)S(1)} %get-tuple-element.44), channel_id=1, source_target_pairs={{0,1},{1,0},{2,3},{3,2},{4,5},{5,4},{6,7},{7,6},{8,9},{9,8},{10,11... | collective-permute-start | bytes 98312 | tf_op jit(solution)/shard_map/ppermute | solution.py:360
  15.0 1.3 %collective-permute-done.5.refs_0_ = f32[16,512]{1,0:T(8,128)S(1)} collective-permute-done((f32[16,512]{1,0:T(8,128)S(1)}, f32[16,512]{1,0:T(8,128)S(1)}, u32[]{:S(2)}, u32[]{:S(2)}) %collective-permute-start.5) | collective-permute-done | bytes 32800 | tf_op jit(solution)/shard_map/ppermute | solution.py:360
  16.4 2.9 %collective-permute-done.6.refs_1_ = f32[16,512]{1,0:T(8,128)S(1)} collective-permute-done((f32[16,512]{1,0:T(8,128)S(1)}, f32[16,512]{1,0:T(8,128)S(1)}, u32[]{:S(2)}, u32[]{:S(2)}) %collective-permute-start.6) | collective-permute-done | bytes 32800 | tf_op jit(solution)/shard_map/ppermute | solution.py:360
  19.3 0.0 collective-permute-done.7.refs_2_
  19.3 0.7 %prior.1 = f32[16,4,512]{2,1,0:T(4,128)} custom-call(f32[16,512]{1,0:T(8,128)S(1)} %collective-permute-done.5.refs_0_, f32[16,512]{1,0:T(8,128)S(1)} %collective-permute-done.6.refs_1_, f32[16,512]{1,0:T(8,128)S(1)} %collective-permute-done.7.refs_2_, f32[16,512]{1,0:T(8,128)S(1)} %get-tuple-element.45.refs_3_, f32[8,512]{1,0:T(8,128)S(1)} %get-tuple-element.46.refs_4_), custom_call_target="tpu_custom_call" | custom-call | tf_op jit(solution)/shard_map/prior/pallas_call | solution.py:456
Async XLA Ops:
  0.0 2.2 %collective-permute-start = (f32[8,4,32]{2,1,0:T(4,128)}, f32[8,4,32]{2,1,0:T(4,128)S(1)}, u32[]{:S(2)}, u32[]{:S(2)}) collective-permute-start(f32[8,4,32]{2,1,0:T(4,128)} %bitcast.4), channel_id=1, source_target_pairs={{4,0},{12,8},{20,16},{28,24},{0,4},{8,12},{16,20},{24,28},{5,1},{1... | collective-permute-start | bytes 12296 | tf_op jit(solution)/shard_map/ppermute | solution.py:369
  2.7 7.1 %collective-permute-start.2 = (f32[21,512]{1,0:T(8,128)S(1)}, f32[21,512]{1,0:T(8,128)S(1)}, u32[]{:S(2)}, u32[]{:S(2)}) collective-permute-start(f32[21,512]{1,0:T(8,128)S(1)} %get-tuple-element.37), channel_id=1, source_target_pairs={{4,8},{12,16},{20,24},{28,0},{8,4},{16,12},{24,20},{0,28},{5,9},{1... | collective-permute-start | bytes 129032 | tf_op jit(solution)/shard_map/ppermute | solution.py:369
  6.4 3.5 %collective-permute-start.1 = (f32[17,512]{1,0:T(8,128)S(1)}, f32[17,512]{1,0:T(8,128)S(1)}, u32[]{:S(2)}, u32[]{:S(2)}) collective-permute-start(f32[17,512]{1,0:T(8,128)S(1)} %get-tuple-element.36), channel_id=1, source_target_pairs={{4,0},{12,8},{20,16},{28,24},{0,4},{8,12},{16,20},{24,28},{5,1},{1... | collective-permute-start | bytes 104456 | tf_op jit(solution)/shard_map/ppermute | solution.py:369
  6.4 3.0 %collective-permute-start.4 = (f32[4,192]{1,0:T(4,128)S(1)}, f32[4,192]{1,0:T(4,128)S(1)}, u32[]{:S(2)}, u32[]{:S(2)}) collective-permute-start(f32[4,192]{1,0:T(4,128)S(1)} %get-tuple-element.41), channel_id=1, source_target_pairs={{4,24},{12,0},{20,8},{28,16},{24,4},{0,12},{8,20},{16,28},{5,25},{... | collective-permute-start | bytes 9224 | tf_op jit(solution)/shard_map/ppermute | solution.py:369
  6.5 3.3 %collective-permute-start.3 = (f32[4,192]{1,0:T(4,128)S(1)}, f32[4,192]{1,0:T(4,128)S(1)}, u32[]{:S(2)}, u32[]{:S(2)}) collective-permute-start(f32[4,192]{1,0:T(4,128)S(1)} %get-tuple-element.38), channel_id=1, source_target_pairs={{4,16},{12,24},{20,0},{28,8},{16,4},{24,12},{0,20},{8,28},{5,17},{... | collective-permute-start | bytes 9224 | tf_op jit(solution)/shard_map/ppermute | solution.py:369
  10.6 5.8 %collective-permute-start.5 = (f32[16,512]{1,0:T(8,128)S(1)}, f32[16,512]{1,0:T(8,128)S(1)}, u32[]{:S(2)}, u32[]{:S(2)}) collective-permute-start(f32[16,512]{1,0:T(8,128)S(1)} %get-tuple-element.42), channel_id=1, source_target_pairs={{0,3},{1,2},{2,1},{3,0},{4,7},{5,6},{6,5},{7,4},{8,11},{9,10},{10,... | collective-permute-start | bytes 98312 | tf_op jit(solution)/shard_map/ppermute | solution.py:360
  14.2 5.0 %collective-permute-start.6 = (f32[16,512]{1,0:T(8,128)S(1)}, f32[16,512]{1,0:T(8,128)S(1)}, u32[]{:S(2)}, u32[]{:S(2)}) collective-permute-start(f32[16,512]{1,0:T(8,128)S(1)} %get-tuple-element.43), channel_id=1, source_target_pairs={{0,2},{1,3},{2,0},{3,1},{4,6},{5,7},{6,4},{7,5},{8,10},{9,11},{10,... | collective-permute-start | bytes 98312 | tf_op jit(solution)/shard_map/ppermute | solution.py:360
  14.2 5.0 %collective-permute-start.7 = (f32[16,512]{1,0:T(8,128)S(1)}, f32[16,512]{1,0:T(8,128)S(1)}, u32[]{:S(2)}, u32[]{:S(2)}) collective-permute-start(f32[16,512]{1,0:T(8,128)S(1)} %get-tuple-element.44), channel_id=1, source_target_pairs={{0,1},{1,0},{2,3},{3,2},{4,5},{5,4},{6,7},{7,6},{8,9},{9,8},{10,11... | collective-permute-start | bytes 98312 | tf_op jit(solution)/shard_map/ppermute | solution.py:360

commit v5 on v2

--- a/solution.py
+++ b/solution.py
@@ -11,6 +11,7 @@
 VERT = 0.2
 STEPS = 4
 PAD = 8
+CUTS = 5
 VMEM = pltpu.VMEM
 SMEM = pltpu.SMEM
 LIMIT = 32 * 1024 * 1024
@@ -45,12 +46,19 @@
         pltpu.make_async_copy(src, dst, sems.at[i])
         for i, (src, dst) in enumerate((
             (damping, damping_v), (profile, profile_v), (table, table_s), (depth, depth_v),
-            (band, band_v), (residual, own), (eta, eta_v), (flow, flow_v),
+            (band, band_v), (residual, own),
         ))
     ]
     for copy in copies:
         copy.start()
-    for copy in copies[:-2]:
+    step = -(-eta.shape[1] // CUTS)
+    large = []
+    for i in range(CUTS):
+        for j, (src, dst) in enumerate(((eta, eta_v), (flow, flow_v))):
+            cut = pl.ds(step * i, min(step, eta.shape[1] - step * i))
+            large.append(pltpu.make_async_copy(src.at[:, cut], dst.at[:, cut], sems.at[len(copies) + 2 * i + j]))
+            large[-1].start()
+    for copy in copies:
         copy.wait()
 
     classes = depth_v[...]
@@ -103,7 +111,7 @@
     w_eta[...] = matrix(us)
     w_flow[...] = matrix(vs)
 
-    for copy in copies[-2:]:
+    for copy in large:
         copy.wait()
 
 
@@ -384,7 +392,7 @@
             VMEM((1, levels), jnp.float32),
             VMEM((1, levels), jnp.float32),
             VMEM((1, band_weight.shape[0]), jnp.float32),
-            pltpu.SemaphoreType.DMA((8,)),
+            pltpu.SemaphoreType.DMA((6 + 2 * CUTS,)),
         ],
         compiler_params=params,
         cost_estimate=pl.CostEstimate(flops=10**7, bytes_accessed=4 * 10**6, transcendentals=0),

time: 20.1 us -> 20.2 us (level)
  transfers between devices with their start and end apart: 8 -> 8, of which waited for: 4 -> 4; matrix products, arithmetic and copies ran while one was open for 0% -> 0% of each run, Pallas kernels for 16% -> 17%
where the time goes in v5:
time: 20.2 us; the launch traced here: 20 us
  starting transfers between devices  9.34 us (46%)
  waiting for transfers between devices  5.35 us (26%)
  Pallas kernels  5.27 us (26%)
    ppermute x5, starting transfers between devices, meet(): return lax.ppermute(x, 'trench', pairs + [(j, i) for i, j in pairs])  4.88 us
    ppermute x3, starting transfers between devices, swaps(): lax.ppermute(parts[r], axis, [(i, i ^ r) for i in range(devices)])  4.45 us
    ppermute x3, waiting for transfers between devices, swaps(): lax.ppermute(parts[r], axis, [(i, i ^ r) for i in range(devices)])  4.09 us
    pallas_call x1, Pallas kernels, body(): pl.pallas_call(prepare_kernel, out_shape=(matrix, matrix, shape(rows, acr...  1.79 us
    ppermute x5, waiting for transfers between devices, meet(): return lax.ppermute(x, 'trench', pairs + [(j, i) for i, j in pairs])  1.26 us
    pallas_call x1, Pallas kernels, body(): pl.pallas_call(functools.partial(sensors_kernel, rows), out_shape=slot_sh...  1.07 us
    pallas_call x1, Pallas kernels, body(): pl.pallas_call(prior_kernel, out_shape=shape(STEPS * blocks, rows // bloc...  0.74 us
    pallas_call x1, Pallas kernels, body(): pl.pallas_call(functools.partial(advance_kernel, tiles), out_shape=(shape...  0.62 us
  transfers between devices with their start and end apart: 8, of which 4 were waited for; matrix products, arithmetic and copies ran while one was open for 0% of the time, Pallas kernels for 17%

profile of v5, /device:TPU:0, one launch (start us, length us, event | category | flops | bytes accessed | tf_op | source)
XLA Modules:
  0.0 20.0 jit_solution(3221494505349516835)
XLA Ops:
  0.0 0.5 %collective-permute-start = (f32[8,4,32]{2,1,0:T(4,128)}, f32[8,4,32]{2,1,0:T(4,128)S(1)}, u32[]{:S(2)}, u32[]{:S(2)}) collective-permute-start(f32[8,4,32]{2,1,0:T(4,128)} %bitcast.4), channel_id=1, source_target_pairs={{4,0},{12,8},{20,16},{28,24},{0,4},{8,12},{16,20},{24,28},{5,1},{1... | collective-permute-start | bytes 12296 | tf_op jit(solution)/shard_map/ppermute | solution.py:371
  0.5 1.8 %prepare.1 = (bf16[192,240]{1,0:T(8,128)(2,1)S(1)}, bf16[192,240]{1,0:T(8,128)(2,1)S(1)}, f32[16,512]{1,0:T(8,128)S(1)}, f32[32,512]{1,0:T(8,128)S(1)}, f32[8,51...) custom-call(s32[16,512]{1,0:T(8,128)} %depth.1, ...), custom_call_target="tpu_custom_call" | custom-call | flops 10000000 | bytes 4000000 | tf_op jit(solution)/shard_map/prepare/pallas_call | solution.py:375
  2.2 0.0 collective-permute-done.partner
  2.3 0.0 copy-start
  2.3 0.6 %contract.1 = (f32[11,16,512]{2,1,0:T(8,128)S(1)}, f32[17,512]{1,0:T(8,128)S(1)}, f32[21,512]{1,0:T(8,128)S(1)}, f32[4,192]{1,0:T(4,128)S(1)}, f32[4,192]{1,0:T(4,128)S(1)}) custom-call(f32[1,30,16,512]{3,2,1,0:T(8,128)S(1)} %get-tuple-element.26.eta, f32[1,30,16,512]{3,2,1,0:T(8,128)S(1)} %get-tuple-element.27.flow, ...), custom_call_target="tpu_custom_call" | custom-call | flops 1000000000 | bytes 4000000 | tf_op jit(solution)/shard_map/contract/pallas_call | solution.py:409
  2.8 0.0 copy-start.1
  2.9 3.6 %collective-permute-start.2 = (f32[21,512]{1,0:T(8,128)S(1)}, f32[21,512]{1,0:T(8,128)S(1)}, u32[]{:S(2)}, u32[]{:S(2)}) collective-permute-start(f32[21,512]{1,0:T(8,128)S(1)} %get-tuple-element.37), channel_id=1, source_target_pairs={{4,8},{12,16},{20,24},{28,0},{8,4},{16,12},{24,20},{0,28},{5,9},{1... | collective-permute-start | bytes 129032 | tf_op jit(solution)/shard_map/ppermute | solution.py:371
  6.5 0.0 collective-permute-start.1
  6.5 0.6 %collective-permute-start.4 = (f32[4,192]{1,0:T(4,128)S(1)}, f32[4,192]{1,0:T(4,128)S(1)}, u32[]{:S(2)}, u32[]{:S(2)}) collective-permute-start(f32[4,192]{1,0:T(4,128)S(1)} %get-tuple-element.41), channel_id=1, source_target_pairs={{4,16},{12,24},{20,0},{28,8},{16,4},{24,12},{0,20},{8,28},{5,17},{... | collective-permute-start | bytes 9224 | tf_op jit(solution)/shard_map/ppermute | solution.py:371
  7.1 0.2 %collective-permute-start.3 = (f32[4,192]{1,0:T(4,128)S(1)}, f32[4,192]{1,0:T(4,128)S(1)}, u32[]{:S(2)}, u32[]{:S(2)}) collective-permute-start(f32[4,192]{1,0:T(4,128)S(1)} %get-tuple-element.38), channel_id=1, source_target_pairs={{4,24},{12,0},{20,8},{28,16},{24,4},{0,12},{8,20},{16,28},{5,25},{... | collective-permute-start | bytes 9224 | tf_op jit(solution)/shard_map/ppermute | solution.py:371
  7.3 1.1 %sensors.1 = (bf16[512,576]{1,0:T(8,128)(2,1)S(1)}, s32[8,576]{1,0:T(8,128)S(1)}, bf16[512,192]{1,0:T(8,128)(2,1)S(1)}, s32[8,192]{1,0:T(8,128)S(1)}) custom-call(s32[8,8,32]{2,1,0:T(8,128)S(1)} %copy-done, s32[8,8]{1,0:T(8,128)S(1)} %copy-done.1), custom_call_target="tpu_custom_call" | custom-call | flops 1000000 | bytes 2000000 | tf_op jit(solution)/shard_map/sensors/pallas_call | solution.py:429
  8.4 1.1 %collective-permute-done.4.refs_1_ = f32[4,192]{1,0:T(4,128)S(1)} collective-permute-done((f32[4,192]{1,0:T(4,128)S(1)}, f32[4,192]{1,0:T(4,128)S(1)}, u32[]{:S(2)}, u32[]{:S(2)}) %collective-permute-start.4) | collective-permute-done | bytes 3104 | tf_op jit(solution)/shard_map/ppermute | solution.py:371
  9.5 0.0 collective-permute-done.2.refs_0_.facing_out
  9.5 0.5 %inject.1.planes = f32[128,512]{1,0:T(8,128)S(1)} custom-call(bf16[512,576]{1,0:T(8,128)(2,1)S(1)} %get-tuple-element.39.hot, s32[8,576]{1,0:T(8,128)S(1)} %get-tuple-element.40.places, f32[8,4,32]{2,1,0:T(4,128)S(1)} %get-tuple-element.31.own, f32[8,4,32]{2,1,0:T(4,128)S(1)} %collective-permute-done.partner, ...), custom_call_target="tpu_custom_call" | custom-call | flops 1000 | bytes 1000 | tf_op jit(solution)/shard_map/inject/pallas_call | solution.py:438
  10.0 0.1 collective-permute-done.3.last
  10.1 0.0 collective-permute-done.1.facing_in
  10.1 0.6 %advance.1 = (f32[16,512]{1,0:T(8,128)S(1)}, f32[16,512]{1,0:T(8,128)S(1)}, f32[16,512]{1,0:T(8,128)S(1)}, f32[16,512]{1,0:T(8,128)S(1)}) custom-call(f32[11,16,512]{2,1,0:T(8,128)S(1)} %get-tuple-element.32.fields, f32[16,512]{1,0:T(8,128)S(1)} %get-tuple-element.30.cel, f32[32,512]{1,0:T(8,128)S(1)} %get-tuple-element.33.coef, ...), custom_call_target="tpu_custom_call" | custom-call | tf_op jit(solution)/shard_map/advance/pallas_call | solution.py:447
  10.7 3.7 %collective-permute-start.5 = (f32[16,512]{1,0:T(8,128)S(1)}, f32[16,512]{1,0:T(8,128)S(1)}, u32[]{:S(2)}, u32[]{:S(2)}) collective-permute-start(f32[16,512]{1,0:T(8,128)S(1)} %get-tuple-element.42), channel_id=1, source_target_pairs={{0,3},{1,2},{2,1},{3,0},{4,7},{5,6},{6,5},{7,4},{8,11},{9,10},{10,... | collective-permute-start | bytes 98312 | tf_op jit(solution)/shard_map/ppermute | solution.py:362
  14.4 0.0 collective-permute-start.6
  14.4 0.8 %collective-permute-start.7 = (f32[16,512]{1,0:T(8,128)S(1)}, f32[16,512]{1,0:T(8,128)S(1)}, u32[]{:S(2)}, u32[]{:S(2)}) collective-permute-start(f32[16,512]{1,0:T(8,128)S(1)} %get-tuple-element.44), channel_id=1, source_target_pairs={{0,1},{1,0},{2,3},{3,2},{4,5},{5,4},{6,7},{7,6},{8,9},{9,8},{10,11... | collective-permute-start | bytes 98312 | tf_op jit(solution)/shard_map/ppermute | solution.py:362
  15.2 1.6 %collective-permute-done.5.refs_0_ = f32[16,512]{1,0:T(8,128)S(1)} collective-permute-done((f32[16,512]{1,0:T(8,128)S(1)}, f32[16,512]{1,0:T(8,128)S(1)}, u32[]{:S(2)}, u32[]{:S(2)}) %collective-permute-start.5) | collective-permute-done | bytes 32800 | tf_op jit(solution)/shard_map/ppermute | solution.py:362
  16.8 2.5 %collective-permute-done.6.refs_1_ = f32[16,512]{1,0:T(8,128)S(1)} collective-permute-done((f32[16,512]{1,0:T(8,128)S(1)}, f32[16,512]{1,0:T(8,128)S(1)}, u32[]{:S(2)}, u32[]{:S(2)}) %collective-permute-start.6) | collective-permute-done | bytes 32800 | tf_op jit(solution)/shard_map/ppermute | solution.py:362
  19.3 0.0 collective-permute-done.7.refs_2_
  19.3 0.7 %prior.1 = f32[16,4,512]{2,1,0:T(4,128)} custom-call(f32[16,512]{1,0:T(8,128)S(1)} %collective-permute-done.5.refs_0_, f32[16,512]{1,0:T(8,128)S(1)} %collective-permute-done.6.refs_1_, f32[16,512]{1,0:T(8,128)S(1)} %collective-permute-done.7.refs_2_, f32[16,512]{1,0:T(8,128)S(1)} %get-tuple-element.45.refs_3_, f32[8,512]{1,0:T(8,128)S(1)} %get-tuple-element.46.refs_4_), custom_call_target="tpu_custom_call" | custom-call | tf_op jit(solution)/shard_map/prior/pallas_call | solution.py:461
  (2 shorter events, 0.0 us)
Async XLA Ops:
  0.0 2.3 %collective-permute-start = (f32[8,4,32]{2,1,0:T(4,128)}, f32[8,4,32]{2,1,0:T(4,128)S(1)}, u32[]{:S(2)}, u32[]{:S(2)}) collective-permute-start(f32[8,4,32]{2,1,0:T(4,128)} %bitcast.4), channel_id=1, source_target_pairs={{4,0},{12,8},{20,16},{28,24},{0,4},{8,12},{16,20},{24,28},{5,1},{1... | collective-permute-start | bytes 12296 | tf_op jit(solution)/shard_map/ppermute | solution.py:371
  2.3 5.0 %copy-start = (s32[8,8,32]{2,1,0:T(8,128)S(1)}, s32[8,8,32]{2,1,0:T(8,128)}, u32[]{:S(2)}) copy-start(s32[8,8,32]{2,1,0:T(8,128)} %cells.1) | copy-start | bytes 24580
  2.8 4.5 %copy-start.1 = (s32[8,8]{1,0:T(8,128)S(1)}, s32[8,8]{1,0:T(8,128)}, u32[]{:S(2)}) copy-start(s32[8,8]{1,0:T(8,128)} %count.1) | copy-start | bytes 772
  2.9 6.6 %collective-permute-start.2 = (f32[21,512]{1,0:T(8,128)S(1)}, f32[21,512]{1,0:T(8,128)S(1)}, u32[]{:S(2)}, u32[]{:S(2)}) collective-permute-start(f32[21,512]{1,0:T(8,128)S(1)} %get-tuple-element.37), channel_id=1, source_target_pairs={{4,8},{12,16},{20,24},{28,0},{8,4},{16,12},{24,20},{0,28},{5,9},{1... | collective-permute-start | bytes 129032 | tf_op jit(solution)/shard_map/ppermute | solution.py:371
  6.5 3.7 %collective-permute-start.1 = (f32[17,512]{1,0:T(8,128)S(1)}, f32[17,512]{1,0:T(8,128)S(1)}, u32[]{:S(2)}, u32[]{:S(2)}) collective-permute-start(f32[17,512]{1,0:T(8,128)S(1)} %get-tuple-element.36), channel_id=1, source_target_pairs={{4,0},{12,8},{20,16},{28,24},{0,4},{8,12},{16,20},{24,28},{5,1},{1... | collective-permute-start | bytes 104456 | tf_op jit(solution)/shard_map/ppermute | solution.py:371
  6.5 3.0 %collective-permute-start.4 = (f32[4,192]{1,0:T(4,128)S(1)}, f32[4,192]{1,0:T(4,128)S(1)}, u32[]{:S(2)}, u32[]{:S(2)}) collective-permute-start(f32[4,192]{1,0:T(4,128)S(1)} %get-tuple-element.41), channel_id=1, source_target_pairs={{4,16},{12,24},{20,0},{28,8},{16,4},{24,12},{0,20},{8,28},{5,17},{... | collective-permute-start | bytes 9224 | tf_op jit(solution)/shard_map/ppermute | solution.py:371
  7.1 3.0 %collective-permute-start.3 = (f32[4,192]{1,0:T(4,128)S(1)}, f32[4,192]{1,0:T(4,128)S(1)}, u32[]{:S(2)}, u32[]{:S(2)}) collective-permute-start(f32[4,192]{1,0:T(4,128)S(1)} %get-tuple-element.38), channel_id=1, source_target_pairs={{4,24},{12,0},{20,8},{28,16},{24,4},{0,12},{8,20},{16,28},{5,25},{... | collective-permute-start | bytes 9224 | tf_op jit(solution)/shard_map/ppermute | solution.py:371
  10.7 6.1 %collective-permute-start.5 = (f32[16,512]{1,0:T(8,128)S(1)}, f32[16,512]{1,0:T(8,128)S(1)}, u32[]{:S(2)}, u32[]{:S(2)}) collective-permute-start(f32[16,512]{1,0:T(8,128)S(1)} %get-tuple-element.42), channel_id=1, source_target_pairs={{0,3},{1,2},{2,1},{3,0},{4,7},{5,6},{6,5},{7,4},{8,11},{9,10},{10,... | collective-permute-start | bytes 98312 | tf_op jit(solution)/shard_map/ppermute | solution.py:362
  14.4 4.9 %collective-permute-start.6 = (f32[16,512]{1,0:T(8,128)S(1)}, f32[16,512]{1,0:T(8,128)S(1)}, u32[]{:S(2)}, u32[]{:S(2)}) collective-permute-start(f32[16,512]{1,0:T(8,128)S(1)} %get-tuple-element.43), channel_id=1, source_target_pairs={{0,2},{1,3},{2,0},{3,1},{4,6},{5,7},{6,4},{7,5},{8,10},{9,11},{10,... | collective-permute-start | bytes 98312 | tf_op jit(solution)/shard_map/ppermute | solution.py:362
  14.4 4.9 %collective-permute-start.7 = (f32[16,512]{1,0:T(8,128)S(1)}, f32[16,512]{1,0:T(8,128)S(1)}, u32[]{:S(2)}, u32[]{:S(2)}) collective-permute-start(f32[16,512]{1,0:T(8,128)S(1)} %get-tuple-element.44), channel_id=1, source_target_pairs={{0,1},{1,0},{2,3},{3,2},{4,5},{5,4},{6,7},{7,6},{8,9},{9,8},{10,11... | collective-permute-start | bytes 98312 | tf_op jit(solution)/shard_map/ppermute | solution.py:362

commit v6 on v2

--- a/solution.py
+++ b/solution.py
@@ -48,7 +48,7 @@
             (band, band_v), (residual, own), (eta, eta_v), (flow, flow_v),
         ))
     ]
-    for copy in copies:
+    for copy in copies[:2] + copies[-2:] + copies[2:-2]:
         copy.start()
     for copy in copies[:-2]:
         copy.wait()

time: 20.1 us -> 20.5 us (1.020)
  Pallas kernels: 5.13 us -> 5.47 us
    pallas_call x1, Pallas kernels: 1.65 us -> 1.99 us  [body(): pl.pallas_call(prepare_kernel, out_shape=(matrix, matrix, shape(rows, acr...]
  transfers between devices with their start and end apart: 8 -> 8, of which waited for: 4 -> 4; matrix products, arithmetic and copies ran while one was open for 0% -> 0% of each run, Pallas kernels for 16% -> 18%
where the time goes in v6:
time: 20.5 us; the launch traced here: 20.2 us
  starting transfers between devices  9.34 us (46%)
  Pallas kernels  5.47 us (27%)
  waiting for transfers between devices  5.35 us (26%)
    ppermute x5, starting transfers between devices, meet(): return lax.ppermute(x, 'trench', pairs + [(j, i) for i, j in pairs])  4.88 us
    ppermute x3, starting transfers between devices, swaps(): lax.ppermute(parts[r], axis, [(i, i ^ r) for i in range(devices)])  4.45 us
    ppermute x3, waiting for transfers between devices, swaps(): lax.ppermute(parts[r], axis, [(i, i ^ r) for i in range(devices)])  4.09 us
    pallas_call x1, Pallas kernels, body(): pl.pallas_call(prepare_kernel, out_shape=(matrix, matrix, shape(rows, acr...  1.99 us
    ppermute x5, waiting for transfers between devices, meet(): return lax.ppermute(x, 'trench', pairs + [(j, i) for i, j in pairs])  1.26 us
    pallas_call x1, Pallas kernels, body(): pl.pallas_call(functools.partial(sensors_kernel, rows), out_shape=slot_sh...  1.07 us
    pallas_call x1, Pallas kernels, body(): pl.pallas_call(prior_kernel, out_shape=shape(STEPS * blocks, rows // bloc...  0.74 us
    pallas_call x1, Pallas kernels, body(): pl.pallas_call(functools.partial(advance_kernel, tiles), out_shape=(shape...  0.62 us
  transfers between devices with their start and end apart: 8, of which 4 were waited for; matrix products, arithmetic and copies ran while one was open for 0% of the time, Pallas kernels for 18%

profile of v6, /device:TPU:0, one launch (start us, length us, event | category | flops | bytes accessed | tf_op | source)
XLA Modules:
  0.0 20.2 jit_solution(5888047858033666119)
XLA Ops:
  0.0 0.5 %collective-permute-start = (f32[8,4,32]{2,1,0:T(4,128)}, f32[8,4,32]{2,1,0:T(4,128)S(1)}, u32[]{:S(2)}, u32[]{:S(2)}) collective-permute-start(f32[8,4,32]{2,1,0:T(4,128)} %bitcast.4), channel_id=1, source_target_pairs={{4,0},{12,8},{20,16},{28,24},{0,4},{8,12},{16,20},{24,28},{5,1},{1... | collective-permute-start | bytes 12296 | tf_op jit(solution)/shard_map/ppermute | solution.py:363
  0.5 2.0 %prepare.1 = (bf16[192,240]{1,0:T(8,128)(2,1)S(1)}, bf16[192,240]{1,0:T(8,128)(2,1)S(1)}, f32[16,512]{1,0:T(8,128)S(1)}, f32[32,512]{1,0:T(8,128)S(1)}, f32[8,51...) custom-call(s32[16,512]{1,0:T(8,128)} %depth.1, ...), custom_call_target="tpu_custom_call" | custom-call | flops 10000000 | bytes 4000000 | tf_op jit(solution)/shard_map/prepare/pallas_call | solution.py:367
  2.5 0.0 collective-permute-done.partner
  2.5 0.0 copy-start
  2.5 0.6 %contract.1 = (f32[11,16,512]{2,1,0:T(8,128)S(1)}, f32[17,512]{1,0:T(8,128)S(1)}, f32[21,512]{1,0:T(8,128)S(1)}, f32[4,192]{1,0:T(4,128)S(1)}, f32[4,192]{1,0:T(4,128)S(1)}) custom-call(f32[1,30,16,512]{3,2,1,0:T(8,128)S(1)} %get-tuple-element.26.eta, f32[1,30,16,512]{3,2,1,0:T(8,128)S(1)} %get-tuple-element.27.flow, ...), custom_call_target="tpu_custom_call" | custom-call | flops 1000000000 | bytes 4000000 | tf_op jit(solution)/shard_map/contract/pallas_call | solution.py:401
  3.0 0.0 copy-start.1
  3.1 3.6 %collective-permute-start.2 = (f32[21,512]{1,0:T(8,128)S(1)}, f32[21,512]{1,0:T(8,128)S(1)}, u32[]{:S(2)}, u32[]{:S(2)}) collective-permute-start(f32[21,512]{1,0:T(8,128)S(1)} %get-tuple-element.37), channel_id=1, source_target_pairs={{4,8},{12,16},{20,24},{28,0},{8,4},{16,12},{24,20},{0,28},{5,9},{1... | collective-permute-start | bytes 129032 | tf_op jit(solution)/shard_map/ppermute | solution.py:363
  6.7 0.0 collective-permute-start.1
  6.7 0.6 %collective-permute-start.4 = (f32[4,192]{1,0:T(4,128)S(1)}, f32[4,192]{1,0:T(4,128)S(1)}, u32[]{:S(2)}, u32[]{:S(2)}) collective-permute-start(f32[4,192]{1,0:T(4,128)S(1)} %get-tuple-element.41), channel_id=1, source_target_pairs={{4,16},{12,24},{20,0},{28,8},{16,4},{24,12},{0,20},{8,28},{5,17},{... | collective-permute-start | bytes 9224 | tf_op jit(solution)/shard_map/ppermute | solution.py:363
  7.3 0.2 collective-permute-start.3
  7.5 1.1 %sensors.1 = (bf16[512,576]{1,0:T(8,128)(2,1)S(1)}, s32[8,576]{1,0:T(8,128)S(1)}, bf16[512,192]{1,0:T(8,128)(2,1)S(1)}, s32[8,192]{1,0:T(8,128)S(1)}) custom-call(s32[8,8,32]{2,1,0:T(8,128)S(1)} %copy-done, s32[8,8]{1,0:T(8,128)S(1)} %copy-done.1), custom_call_target="tpu_custom_call" | custom-call | flops 1000000 | bytes 2000000 | tf_op jit(solution)/shard_map/sensors/pallas_call | solution.py:421
  8.6 1.1 %collective-permute-done.4.refs_1_ = f32[4,192]{1,0:T(4,128)S(1)} collective-permute-done((f32[4,192]{1,0:T(4,128)S(1)}, f32[4,192]{1,0:T(4,128)S(1)}, u32[]{:S(2)}, u32[]{:S(2)}) %collective-permute-start.4) | collective-permute-done | bytes 3104 | tf_op jit(solution)/shard_map/ppermute | solution.py:363
  9.7 0.0 collective-permute-done.2.refs_0_.facing_out
  9.7 0.5 %inject.1.planes = f32[128,512]{1,0:T(8,128)S(1)} custom-call(bf16[512,576]{1,0:T(8,128)(2,1)S(1)} %get-tuple-element.39.hot, s32[8,576]{1,0:T(8,128)S(1)} %get-tuple-element.40.places, f32[8,4,32]{2,1,0:T(4,128)S(1)} %get-tuple-element.31.own, f32[8,4,32]{2,1,0:T(4,128)S(1)} %collective-permute-done.partner, ...), custom_call_target="tpu_custom_call" | custom-call | flops 1000 | bytes 1000 | tf_op jit(solution)/shard_map/inject/pallas_call | solution.py:430
  10.2 0.1 collective-permute-done.3.last
  10.3 0.0 collective-permute-done.1.facing_in
  10.3 0.6 %advance.1 = (f32[16,512]{1,0:T(8,128)S(1)}, f32[16,512]{1,0:T(8,128)S(1)}, f32[16,512]{1,0:T(8,128)S(1)}, f32[16,512]{1,0:T(8,128)S(1)}) custom-call(f32[11,16,512]{2,1,0:T(8,128)S(1)} %get-tuple-element.32.fields, f32[16,512]{1,0:T(8,128)S(1)} %get-tuple-element.30.cel, f32[32,512]{1,0:T(8,128)S(1)} %get-tuple-element.33.coef, ...), custom_call_target="tpu_custom_call" | custom-call | tf_op jit(solution)/shard_map/advance/pallas_call | solution.py:439
  11.0 3.7 %collective-permute-start.5 = (f32[16,512]{1,0:T(8,128)S(1)}, f32[16,512]{1,0:T(8,128)S(1)}, u32[]{:S(2)}, u32[]{:S(2)}) collective-permute-start(f32[16,512]{1,0:T(8,128)S(1)} %get-tuple-element.42), channel_id=1, source_target_pairs={{0,3},{1,2},{2,1},{3,0},{4,7},{5,6},{6,5},{7,4},{8,11},{9,10},{10,... | collective-permute-start | bytes 98312 | tf_op jit(solution)/shard_map/ppermute | solution.py:354
  14.6 0.0 collective-permute-start.6
  14.6 0.8 %collective-permute-start.7 = (f32[16,512]{1,0:T(8,128)S(1)}, f32[16,512]{1,0:T(8,128)S(1)}, u32[]{:S(2)}, u32[]{:S(2)}) collective-permute-start(f32[16,512]{1,0:T(8,128)S(1)} %get-tuple-element.44), channel_id=1, source_target_pairs={{0,1},{1,0},{2,3},{3,2},{4,5},{5,4},{6,7},{7,6},{8,9},{9,8},{10,11... | collective-permute-start | bytes 98312 | tf_op jit(solution)/shard_map/ppermute | solution.py:354
  15.4 1.6 %collective-permute-done.5.refs_0_ = f32[16,512]{1,0:T(8,128)S(1)} collective-permute-done((f32[16,512]{1,0:T(8,128)S(1)}, f32[16,512]{1,0:T(8,128)S(1)}, u32[]{:S(2)}, u32[]{:S(2)}) %collective-permute-start.5) | collective-permute-done | bytes 32800 | tf_op jit(solution)/shard_map/ppermute | solution.py:354
  17.0 2.5 %collective-permute-done.6.refs_1_ = f32[16,512]{1,0:T(8,128)S(1)} collective-permute-done((f32[16,512]{1,0:T(8,128)S(1)}, f32[16,512]{1,0:T(8,128)S(1)}, u32[]{:S(2)}, u32[]{:S(2)}) %collective-permute-start.6) | collective-permute-done | bytes 32800 | tf_op jit(solution)/shard_map/ppermute | solution.py:354
  19.5 0.0 collective-permute-done.7.refs_2_
  19.5 0.7 %prior.1 = f32[16,4,512]{2,1,0:T(4,128)} custom-call(f32[16,512]{1,0:T(8,128)S(1)} %collective-permute-done.5.refs_0_, f32[16,512]{1,0:T(8,128)S(1)} %collective-permute-done.6.refs_1_, f32[16,512]{1,0:T(8,128)S(1)} %collective-permute-done.7.refs_2_, f32[16,512]{1,0:T(8,128)S(1)} %get-tuple-element.45.refs_3_, f32[8,512]{1,0:T(8,128)S(1)} %get-tuple-element.46.refs_4_), custom_call_target="tpu_custom_call" | custom-call | tf_op jit(solution)/shard_map/prior/pallas_call | solution.py:453
  (2 shorter events, 0.0 us)
Async XLA Ops:
  0.0 2.5 %collective-permute-start = (f32[8,4,32]{2,1,0:T(4,128)}, f32[8,4,32]{2,1,0:T(4,128)S(1)}, u32[]{:S(2)}, u32[]{:S(2)}) collective-permute-start(f32[8,4,32]{2,1,0:T(4,128)} %bitcast.4), channel_id=1, source_target_pairs={{4,0},{12,8},{20,16},{28,24},{0,4},{8,12},{16,20},{24,28},{5,1},{1... | collective-permute-start | bytes 12296 | tf_op jit(solution)/shard_map/ppermute | solution.py:363
  2.5 5.0 %copy-start = (s32[8,8,32]{2,1,0:T(8,128)S(1)}, s32[8,8,32]{2,1,0:T(8,128)}, u32[]{:S(2)}) copy-start(s32[8,8,32]{2,1,0:T(8,128)} %cells.1) | copy-start | bytes 24580
  3.0 4.5 %copy-start.1 = (s32[8,8]{1,0:T(8,128)S(1)}, s32[8,8]{1,0:T(8,128)}, u32[]{:S(2)}) copy-start(s32[8,8]{1,0:T(8,128)} %count.1) | copy-start | bytes 772
  3.1 6.6 %collective-permute-start.2 = (f32[21,512]{1,0:T(8,128)S(1)}, f32[21,512]{1,0:T(8,128)S(1)}, u32[]{:S(2)}, u32[]{:S(2)}) collective-permute-start(f32[21,512]{1,0:T(8,128)S(1)} %get-tuple-element.37), channel_id=1, source_target_pairs={{4,8},{12,16},{20,24},{28,0},{8,4},{16,12},{24,20},{0,28},{5,9},{1... | collective-permute-start | bytes 129032 | tf_op jit(solution)/shard_map/ppermute | solution.py:363
  6.7 3.7 %collective-permute-start.1 = (f32[17,512]{1,0:T(8,128)S(1)}, f32[17,512]{1,0:T(8,128)S(1)}, u32[]{:S(2)}, u32[]{:S(2)}) collective-permute-start(f32[17,512]{1,0:T(8,128)S(1)} %get-tuple-element.36), channel_id=1, source_target_pairs={{4,0},{12,8},{20,16},{28,24},{0,4},{8,12},{16,20},{24,28},{5,1},{1... | collective-permute-start | bytes 104456 | tf_op jit(solution)/shard_map/ppermute | solution.py:363
  6.7 3.0 %collective-permute-start.4 = (f32[4,192]{1,0:T(4,128)S(1)}, f32[4,192]{1,0:T(4,128)S(1)}, u32[]{:S(2)}, u32[]{:S(2)}) collective-permute-start(f32[4,192]{1,0:T(4,128)S(1)} %get-tuple-element.41), channel_id=1, source_target_pairs={{4,16},{12,24},{20,0},{28,8},{16,4},{24,12},{0,20},{8,28},{5,17},{... | collective-permute-start | bytes 9224 | tf_op jit(solution)/shard_map/ppermute | solution.py:363
  7.3 3.0 %collective-permute-start.3 = (f32[4,192]{1,0:T(4,128)S(1)}, f32[4,192]{1,0:T(4,128)S(1)}, u32[]{:S(2)}, u32[]{:S(2)}) collective-permute-start(f32[4,192]{1,0:T(4,128)S(1)} %get-tuple-element.38), channel_id=1, source_target_pairs={{4,24},{12,0},{20,8},{28,16},{24,4},{0,12},{8,20},{16,28},{5,25},{... | collective-permute-start | bytes 9224 | tf_op jit(solution)/shard_map/ppermute | solution.py:363
  11.0 6.1 %collective-permute-start.5 = (f32[16,512]{1,0:T(8,128)S(1)}, f32[16,512]{1,0:T(8,128)S(1)}, u32[]{:S(2)}, u32[]{:S(2)}) collective-permute-start(f32[16,512]{1,0:T(8,128)S(1)} %get-tuple-element.42), channel_id=1, source_target_pairs={{0,3},{1,2},{2,1},{3,0},{4,7},{5,6},{6,5},{7,4},{8,11},{9,10},{10,... | collective-permute-start | bytes 98312 | tf_op jit(solution)/shard_map/ppermute | solution.py:354
  14.6 4.9 %collective-permute-start.6 = (f32[16,512]{1,0:T(8,128)S(1)}, f32[16,512]{1,0:T(8,128)S(1)}, u32[]{:S(2)}, u32[]{:S(2)}) collective-permute-start(f32[16,512]{1,0:T(8,128)S(1)} %get-tuple-element.43), channel_id=1, source_target_pairs={{0,2},{1,3},{2,0},{3,1},{4,6},{5,7},{6,4},{7,5},{8,10},{9,11},{10,... | collective-permute-start | bytes 98312 | tf_op jit(solution)/shard_map/ppermute | solution.py:354
  14.6 4.9 %collective-permute-start.7 = (f32[16,512]{1,0:T(8,128)S(1)}, f32[16,512]{1,0:T(8,128)S(1)}, u32[]{:S(2)}, u32[]{:S(2)}) collective-permute-start(f32[16,512]{1,0:T(8,128)S(1)} %get-tuple-element.44), channel_id=1, source_target_pairs={{0,1},{1,0},{2,3},{3,2},{4,5},{5,4},{6,7},{7,6},{8,9},{9,8},{10,11... | collective-permute-start | bytes 98312 | tf_op jit(solution)/shard_map/ppermute | solution.py:354

commit v7 on v2

--- a/solution.py
+++ b/solution.py
@@ -50,16 +50,8 @@
     ]
     for copy in copies:
         copy.start()
-    for copy in copies[:-2]:
+    for copy in copies[:2]:
         copy.wait()
-
-    classes = depth_v[...]
-    speed = jnp.zeros(classes.shape, jnp.float32)
-    for c in range(table_s.shape[0]):
-        speed = jnp.where(classes == c, table_s[c], speed)
-    cel[...] = speed
-    for j in range(factor.shape[0]):
-        factor[j : j + 1, :] = jnp.broadcast_to(band_v[:, j : j + 1], (1, across))
 
     lane = lax.broadcasted_iota(jnp.int32, (8, 128), 1)
     sub = lax.broadcasted_iota(jnp.int32, (8, 128), 0)
@@ -102,6 +94,17 @@
 
     w_eta[...] = matrix(us)
     w_flow[...] = matrix(vs)
+
+    for copy in copies[2:-2]:
+        copy.wait()
+
+    classes = depth_v[...]
+    speed = jnp.zeros(classes.shape, jnp.float32)
+    for c in range(table_s.shape[0]):
+        speed = jnp.where(classes == c, table_s[c], speed)
+    cel[...] = speed
+    for j in range(factor.shape[0]):
+        factor[j : j + 1, :] = jnp.broadcast_to(band_v[:, j : j + 1], (1, across))
 
     for copy in copies[-2:]:
         copy.wait()

time: 20.1 us -> 20.1 us (level)
  no operation moved by 1% of the time
where the time goes in v7:
time: 20.1 us; the launch traced here: 19.9 us
  starting transfers between devices  9.35 us (47%)
  waiting for transfers between devices  5.34 us (27%)
  Pallas kernels  5.13 us (26%)
    ppermute x5, starting transfers between devices, meet(): return lax.ppermute(x, 'trench', pairs + [(j, i) for i, j in pairs])  4.9 us
    ppermute x3, starting transfers between devices, swaps(): lax.ppermute(parts[r], axis, [(i, i ^ r) for i in range(devices)])  4.45 us
    ppermute x3, waiting for transfers between devices, swaps(): lax.ppermute(parts[r], axis, [(i, i ^ r) for i in range(devices)])  4.09 us
    pallas_call x1, Pallas kernels, body(): pl.pallas_call(prepare_kernel, out_shape=(matrix, matrix, shape(rows, acr...  1.65 us
    ppermute x5, waiting for transfers between devices, meet(): return lax.ppermute(x, 'trench', pairs + [(j, i) for i, j in pairs])  1.25 us
    pallas_call x1, Pallas kernels, body(): pl.pallas_call(functools.partial(sensors_kernel, rows), out_shape=slot_sh...  1.07 us
    pallas_call x1, Pallas kernels, body(): pl.pallas_call(prior_kernel, out_shape=shape(STEPS * blocks, rows // bloc...  0.74 us
    pallas_call x1, Pallas kernels, body(): pl.pallas_call(functools.partial(advance_kernel, tiles), out_shape=(shape...  0.62 us
  transfers between devices with their start and end apart: 8, of which 4 were waited for; matrix products, arithmetic and copies ran while one was open for 0% of the time, Pallas kernels for 16%

profile of v7, /device:TPU:0, one launch (start us, length us, event | category | flops | bytes accessed | tf_op | source)
XLA Modules:
  0.0 19.9 jit_solution(11190382593731072902)
XLA Ops:
  0.0 0.5 %collective-permute-start = (f32[8,4,32]{2,1,0:T(4,128)}, f32[8,4,32]{2,1,0:T(4,128)S(1)}, u32[]{:S(2)}, u32[]{:S(2)}) collective-permute-start(f32[8,4,32]{2,1,0:T(4,128)} %bitcast.4), channel_id=1, source_target_pairs={{4,0},{12,8},{20,16},{28,24},{0,4},{8,12},{16,20},{24,28},{5,1},{1... | collective-permute-start | bytes 12296 | tf_op jit(solution)/shard_map/ppermute | solution.py:366
  0.5 1.7 %prepare.1 = (bf16[192,240]{1,0:T(8,128)(2,1)S(1)}, bf16[192,240]{1,0:T(8,128)(2,1)S(1)}, f32[16,512]{1,0:T(8,128)S(1)}, f32[32,512]{1,0:T(8,128)S(1)}, f32[8,51...) custom-call(s32[16,512]{1,0:T(8,128)} %depth.1, ...), custom_call_target="tpu_custom_call" | custom-call | flops 10000000 | bytes 4000000 | tf_op jit(solution)/shard_map/prepare/pallas_call | solution.py:370
  2.1 0.0 collective-permute-done.partner
  2.1 0.0 copy-start
  2.1 0.6 %contract.1 = (f32[11,16,512]{2,1,0:T(8,128)S(1)}, f32[17,512]{1,0:T(8,128)S(1)}, f32[21,512]{1,0:T(8,128)S(1)}, f32[4,192]{1,0:T(4,128)S(1)}, f32[4,192]{1,0:T(4,128)S(1)}) custom-call(f32[1,30,16,512]{3,2,1,0:T(8,128)S(1)} %get-tuple-element.26.eta, f32[1,30,16,512]{3,2,1,0:T(8,128)S(1)} %get-tuple-element.27.flow, ...), custom_call_target="tpu_custom_call" | custom-call | flops 1000000000 | bytes 4000000 | tf_op jit(solution)/shard_map/contract/pallas_call | solution.py:404
  2.7 0.0 copy-start.1
  2.7 3.6 %collective-permute-start.2 = (f32[21,512]{1,0:T(8,128)S(1)}, f32[21,512]{1,0:T(8,128)S(1)}, u32[]{:S(2)}, u32[]{:S(2)}) collective-permute-start(f32[21,512]{1,0:T(8,128)S(1)} %get-tuple-element.37), channel_id=1, source_target_pairs={{4,8},{12,16},{20,24},{28,0},{8,4},{16,12},{24,20},{0,28},{5,9},{1... | collective-permute-start | bytes 129032 | tf_op jit(solution)/shard_map/ppermute | solution.py:366
  6.3 0.0 collective-permute-start.1
  6.3 0.6 %collective-permute-start.4 = (f32[4,192]{1,0:T(4,128)S(1)}, f32[4,192]{1,0:T(4,128)S(1)}, u32[]{:S(2)}, u32[]{:S(2)}) collective-permute-start(f32[4,192]{1,0:T(4,128)S(1)} %get-tuple-element.41), channel_id=1, source_target_pairs={{4,16},{12,24},{20,0},{28,8},{16,4},{24,12},{0,20},{8,28},{5,17},{... | collective-permute-start | bytes 9224 | tf_op jit(solution)/shard_map/ppermute | solution.py:366
  6.9 0.2 %collective-permute-start.3 = (f32[4,192]{1,0:T(4,128)S(1)}, f32[4,192]{1,0:T(4,128)S(1)}, u32[]{:S(2)}, u32[]{:S(2)}) collective-permute-start(f32[4,192]{1,0:T(4,128)S(1)} %get-tuple-element.38), channel_id=1, source_target_pairs={{4,24},{12,0},{20,8},{28,16},{24,4},{0,12},{8,20},{16,28},{5,25},{... | collective-permute-start | bytes 9224 | tf_op jit(solution)/shard_map/ppermute | solution.py:366
  7.2 1.1 %sensors.1 = (bf16[512,576]{1,0:T(8,128)(2,1)S(1)}, s32[8,576]{1,0:T(8,128)S(1)}, bf16[512,192]{1,0:T(8,128)(2,1)S(1)}, s32[8,192]{1,0:T(8,128)S(1)}) custom-call(s32[8,8,32]{2,1,0:T(8,128)S(1)} %copy-done, s32[8,8]{1,0:T(8,128)S(1)} %copy-done.1), custom_call_target="tpu_custom_call" | custom-call | flops 1000000 | bytes 2000000 | tf_op jit(solution)/shard_map/sensors/pallas_call | solution.py:424
  8.2 1.1 %collective-permute-done.4.refs_1_ = f32[4,192]{1,0:T(4,128)S(1)} collective-permute-done((f32[4,192]{1,0:T(4,128)S(1)}, f32[4,192]{1,0:T(4,128)S(1)}, u32[]{:S(2)}, u32[]{:S(2)}) %collective-permute-start.4) | collective-permute-done | bytes 3104 | tf_op jit(solution)/shard_map/ppermute | solution.py:366
  9.4 0.0 collective-permute-done.2.refs_0_.facing_out
  9.4 0.5 %inject.1.planes = f32[128,512]{1,0:T(8,128)S(1)} custom-call(bf16[512,576]{1,0:T(8,128)(2,1)S(1)} %get-tuple-element.39.hot, s32[8,576]{1,0:T(8,128)S(1)} %get-tuple-element.40.places, f32[8,4,32]{2,1,0:T(4,128)S(1)} %get-tuple-element.31.own, f32[8,4,32]{2,1,0:T(4,128)S(1)} %collective-permute-done.partner, ...), custom_call_target="tpu_custom_call" | custom-call | flops 1000 | bytes 1000 | tf_op jit(solution)/shard_map/inject/pallas_call | solution.py:433
  9.9 0.1 collective-permute-done.3.last
  10.0 0.0 collective-permute-done.1.facing_in
  10.0 0.6 %advance.1 = (f32[16,512]{1,0:T(8,128)S(1)}, f32[16,512]{1,0:T(8,128)S(1)}, f32[16,512]{1,0:T(8,128)S(1)}, f32[16,512]{1,0:T(8,128)S(1)}) custom-call(f32[11,16,512]{2,1,0:T(8,128)S(1)} %get-tuple-element.32.fields, f32[16,512]{1,0:T(8,128)S(1)} %get-tuple-element.30.cel, f32[32,512]{1,0:T(8,128)S(1)} %get-tuple-element.33.coef, ...), custom_call_target="tpu_custom_call" | custom-call | tf_op jit(solution)/shard_map/advance/pallas_call | solution.py:442
  10.6 3.7 %collective-permute-start.5 = (f32[16,512]{1,0:T(8,128)S(1)}, f32[16,512]{1,0:T(8,128)S(1)}, u32[]{:S(2)}, u32[]{:S(2)}) collective-permute-start(f32[16,512]{1,0:T(8,128)S(1)} %get-tuple-element.42), channel_id=1, source_target_pairs={{0,3},{1,2},{2,1},{3,0},{4,7},{5,6},{6,5},{7,4},{8,11},{9,10},{10,... | collective-permute-start | bytes 98312 | tf_op jit(solution)/shard_map/ppermute | solution.py:357
  14.3 0.0 collective-permute-start.6
  14.3 0.8 %collective-permute-start.7 = (f32[16,512]{1,0:T(8,128)S(1)}, f32[16,512]{1,0:T(8,128)S(1)}, u32[]{:S(2)}, u32[]{:S(2)}) collective-permute-start(f32[16,512]{1,0:T(8,128)S(1)} %get-tuple-element.44), channel_id=1, source_target_pairs={{0,1},{1,0},{2,3},{3,2},{4,5},{5,4},{6,7},{7,6},{8,9},{9,8},{10,11... | collective-permute-start | bytes 98312 | tf_op jit(solution)/shard_map/ppermute | solution.py:357
  15.1 1.6 %collective-permute-done.5.refs_0_ = f32[16,512]{1,0:T(8,128)S(1)} collective-permute-done((f32[16,512]{1,0:T(8,128)S(1)}, f32[16,512]{1,0:T(8,128)S(1)}, u32[]{:S(2)}, u32[]{:S(2)}) %collective-permute-start.5) | collective-permute-done | bytes 32800 | tf_op jit(solution)/shard_map/ppermute | solution.py:357
  16.7 2.5 %collective-permute-done.6.refs_1_ = f32[16,512]{1,0:T(8,128)S(1)} collective-permute-done((f32[16,512]{1,0:T(8,128)S(1)}, f32[16,512]{1,0:T(8,128)S(1)}, u32[]{:S(2)}, u32[]{:S(2)}) %collective-permute-start.6) | collective-permute-done | bytes 32800 | tf_op jit(solution)/shard_map/ppermute | solution.py:357
  19.2 0.0 collective-permute-done.7.refs_2_
  19.2 0.7 %prior.1 = f32[16,4,512]{2,1,0:T(4,128)} custom-call(f32[16,512]{1,0:T(8,128)S(1)} %collective-permute-done.5.refs_0_, f32[16,512]{1,0:T(8,128)S(1)} %collective-permute-done.6.refs_1_, f32[16,512]{1,0:T(8,128)S(1)} %collective-permute-done.7.refs_2_, f32[16,512]{1,0:T(8,128)S(1)} %get-tuple-element.45.refs_3_, f32[8,512]{1,0:T(8,128)S(1)} %get-tuple-element.46.refs_4_), custom_call_target="tpu_custom_call" | custom-call | tf_op jit(solution)/shard_map/prior/pallas_call | solution.py:456
  (2 shorter events, 0.0 us)
Async XLA Ops:
  0.0 2.1 %collective-permute-start = (f32[8,4,32]{2,1,0:T(4,128)}, f32[8,4,32]{2,1,0:T(4,128)S(1)}, u32[]{:S(2)}, u32[]{:S(2)}) collective-permute-start(f32[8,4,32]{2,1,0:T(4,128)} %bitcast.4), channel_id=1, source_target_pairs={{4,0},{12,8},{20,16},{28,24},{0,4},{8,12},{16,20},{24,28},{5,1},{1... | collective-permute-start | bytes 12296 | tf_op jit(solution)/shard_map/ppermute | solution.py:366
  2.1 5.0 %copy-start = (s32[8,8,32]{2,1,0:T(8,128)S(1)}, s32[8,8,32]{2,1,0:T(8,128)}, u32[]{:S(2)}) copy-start(s32[8,8,32]{2,1,0:T(8,128)} %cells.1) | copy-start | bytes 24580
  2.7 4.5 %copy-start.1 = (s32[8,8]{1,0:T(8,128)S(1)}, s32[8,8]{1,0:T(8,128)}, u32[]{:S(2)}) copy-start(s32[8,8]{1,0:T(8,128)} %count.1) | copy-start | bytes 772
  2.7 6.7 %collective-permute-start.2 = (f32[21,512]{1,0:T(8,128)S(1)}, f32[21,512]{1,0:T(8,128)S(1)}, u32[]{:S(2)}, u32[]{:S(2)}) collective-permute-start(f32[21,512]{1,0:T(8,128)S(1)} %get-tuple-element.37), channel_id=1, source_target_pairs={{4,8},{12,16},{20,24},{28,0},{8,4},{16,12},{24,20},{0,28},{5,9},{1... | collective-permute-start | bytes 129032 | tf_op jit(solution)/shard_map/ppermute | solution.py:366
  6.3 3.7 %collective-permute-start.1 = (f32[17,512]{1,0:T(8,128)S(1)}, f32[17,512]{1,0:T(8,128)S(1)}, u32[]{:S(2)}, u32[]{:S(2)}) collective-permute-start(f32[17,512]{1,0:T(8,128)S(1)} %get-tuple-element.36), channel_id=1, source_target_pairs={{4,0},{12,8},{20,16},{28,24},{0,4},{8,12},{16,20},{24,28},{5,1},{1... | collective-permute-start | bytes 104456 | tf_op jit(solution)/shard_map/ppermute | solution.py:366
  6.3 3.0 %collective-permute-start.4 = (f32[4,192]{1,0:T(4,128)S(1)}, f32[4,192]{1,0:T(4,128)S(1)}, u32[]{:S(2)}, u32[]{:S(2)}) collective-permute-start(f32[4,192]{1,0:T(4,128)S(1)} %get-tuple-element.41), channel_id=1, source_target_pairs={{4,16},{12,24},{20,0},{28,8},{16,4},{24,12},{0,20},{8,28},{5,17},{... | collective-permute-start | bytes 9224 | tf_op jit(solution)/shard_map/ppermute | solution.py:366
  6.9 3.0 %collective-permute-start.3 = (f32[4,192]{1,0:T(4,128)S(1)}, f32[4,192]{1,0:T(4,128)S(1)}, u32[]{:S(2)}, u32[]{:S(2)}) collective-permute-start(f32[4,192]{1,0:T(4,128)S(1)} %get-tuple-element.38), channel_id=1, source_target_pairs={{4,24},{12,0},{20,8},{28,16},{24,4},{0,12},{8,20},{16,28},{5,25},{... | collective-permute-start | bytes 9224 | tf_op jit(solution)/shard_map/ppermute | solution.py:366
  10.6 6.1 %collective-permute-start.5 = (f32[16,512]{1,0:T(8,128)S(1)}, f32[16,512]{1,0:T(8,128)S(1)}, u32[]{:S(2)}, u32[]{:S(2)}) collective-permute-start(f32[16,512]{1,0:T(8,128)S(1)} %get-tuple-element.42), channel_id=1, source_target_pairs={{0,3},{1,2},{2,1},{3,0},{4,7},{5,6},{6,5},{7,4},{8,11},{9,10},{10,... | collective-permute-start | bytes 98312 | tf_op jit(solution)/shard_map/ppermute | solution.py:357
  14.3 4.9 %collective-permute-start.6 = (f32[16,512]{1,0:T(8,128)S(1)}, f32[16,512]{1,0:T(8,128)S(1)}, u32[]{:S(2)}, u32[]{:S(2)}) collective-permute-start(f32[16,512]{1,0:T(8,128)S(1)} %get-tuple-element.43), channel_id=1, source_target_pairs={{0,2},{1,3},{2,0},{3,1},{4,6},{5,7},{6,4},{7,5},{8,10},{9,11},{10,... | collective-permute-start | bytes 98312 | tf_op jit(solution)/shard_map/ppermute | solution.py:357
  14.3 4.9 %collective-permute-start.7 = (f32[16,512]{1,0:T(8,128)S(1)}, f32[16,512]{1,0:T(8,128)S(1)}, u32[]{:S(2)}, u32[]{:S(2)}) collective-permute-start(f32[16,512]{1,0:T(8,128)S(1)} %get-tuple-element.44), channel_id=1, source_target_pairs={{0,1},{1,0},{2,3},{3,2},{4,5},{5,4},{6,7},{7,6},{8,9},{9,8},{10,11... | collective-permute-start | bytes 98312 | tf_op jit(solution)/shard_map/ppermute | solution.py:357
